TPU v7x, 128 devices: a whole 4x4x4 slice. The times are simulated.
128 devices in a mesh: rows: 64 (over y_lo, x, z, core), sub: 2 (over y_hi).
Axes of the slice: x: 4, y: 4 (y_hi: 2, y_lo: 2; y = y_hi * 2 + y_lo), z: 4, core: 2. Of those that a mesh axis runs over, the one named last changes fastest.
Arguments:
- matrix_rows: float32 [524288, 256], P(('rows', 'sub')), may hold values from -6 to 6
- signs: int32 [524288], P(('rows', 'sub')), may hold values from 0 to 1
- picks: int32 [128, 128, 4], P(('rows', 'sub')), may hold values from -1 to 4095, as said below
Outputs:
- mixed: float32 [524288, 256], P(('rows', 'sub'))
- panel: float32 [65536, 256], P(('rows', 'sub'))
- factor: float32 [256, 256], replicated
Inputs may be any that keep to these rules, and one draw needn't show every extreme that they name: `picks`: -1 marks an empty slot; about half of the slots are filled.
All inputs are finite; a program needn't handle non-finite values.
Results may differ from a plain program's by a relative error of at most 0.000098.
Values sent between devices are 32-bit elements; how exact they have to be, the bound alone decides.
No kernel may reach another device: no remote copies, remote signals or barrier semaphores. Data moves between devices by JAX's collectives and lax.ppermute only.
A program may use at most 64 MiB of HBM per device.

v0:
```python
import math

import jax
import jax.numpy as jnp
from jax import lax
from jax.sharding import PartitionSpec as P


def from_partner(block, axis, stride):
    count = lax.axis_size(axis)
    route = []
    for low in range(count):
        high = low | 1 << stride
        if high != low and high < count:
            route += [(low, high), (high, low)]
    return lax.ppermute(block, axis, route)


def sylvester(order):
    row_index = lax.broadcasted_iota(jnp.int32, (order, order), 0)
    column_index = lax.broadcasted_iota(jnp.int32, (order, order), 1)
    correlation = jnp.bitwise_and(row_index, column_index)
    parity = jnp.zeros((order, order), jnp.int32)
    for level_bit in range(max(order.bit_length() - 1, 0)):
        parity = jnp.bitwise_xor(
            parity, jnp.bitwise_and(jnp.right_shift(correlation, level_bit), 1)
        )
    return (1 - 2 * parity).astype(jnp.float32)


def local_mix(values):
    length = values.shape[0]
    powers = length.bit_length() - 1
    first = 2 ** (powers // 2)
    second = length // first
    blocks = values.reshape(first, second, values.shape[1])
    blocks = jnp.einsum("ij,jbc->ibc", sylvester(first), blocks, precision=lax.Precision.HIGHEST)
    blocks = jnp.einsum("ij,ajc->aic", sylvester(second), blocks, precision=lax.Precision.HIGHEST)
    return blocks.reshape(length, values.shape[1])


def on_device(matrix_rows, signs, picks):
    length = matrix_rows.shape[0]
    width = matrix_rows.shape[1]
    row_count = lax.axis_size("rows")
    owners = row_count * lax.axis_size("sub")
    scale = 1.0 / math.sqrt(length * owners)
    flips = (2 * signs - 1).astype(jnp.float32) * scale
    values = local_mix(matrix_rows * flips[:, None])
    partner = from_partner(values, "sub", 0)
    upper = lax.axis_index("sub")
    values = jnp.where(upper == 1, partner - values, partner + values)
    position = lax.axis_index("rows")
    for level_bit in range(row_count.bit_length() - 1):
        partner = from_partner(values, "rows", level_bit)
        upper = position >> level_bit & 1
        values = jnp.where(upper == 1, partner - values, partner + values)
    slots = picks[0]
    flat_picks = slots.reshape(-1)
    taken = jnp.take(values, jnp.maximum(flat_picks, 0), axis=0)
    taken = jnp.where((flat_picks >= 0)[:, None], taken, jnp.float32(0.0))
    outgoing = taken.reshape(slots.shape[0], slots.shape[1], width)
    received = lax.all_to_all(outgoing, ("rows", "sub"), split_axis=0, concat_axis=0, tiled=True)
    panel = received.reshape(-1, width)
    expected = owners * owners * slots.shape[1] / 2.0
    gram_part = jnp.dot(
        panel.T, panel, precision=lax.Precision.HIGHEST, preferred_element_type=jnp.float32
    )
    gram = lax.psum(gram_part, ("rows", "sub")) / expected
    factor = jnp.linalg.cholesky(gram).T
    return (values, panel, factor)


def solution(mesh):
    placed = (P(("rows", "sub"), None), P(("rows", "sub")), P(("rows", "sub"), None, None))
    return jax.shard_map(
        on_device,
        mesh=mesh,
        in_specs=placed,
        out_specs=(P(("rows", "sub"), None), P(("rows", "sub"), None), P()),
        check_vma=False,
    )
```

profile of v0, /device:TPU:1, one launch (start us, length us, event | category | flops | bytes accessed | tf_op | source)
XLA Modules:
  0.0 841.0 jit_solution(4797206375977581141)
XLA Ops:
  7.2 0.0 all-reduce.3.cloned.1.call-start
  7.2 0.7 convert_multiply_fusion
  7.9 2.6 broadcast_multiply_fusion
  10.5 6.2 fusion.2
  16.8 7.1 fusion
  23.9 3.7 collective-permute-start
  27.6 90.3 %collective-permute-done = f32[4096,256]{1,0:T(8,128)} collective-permute-done((f32[4096,256]{1,0:T(8,128)}, f32[4096,256]{1,0:T(8,128)}, u32[]{:S(2)}, u32[]{:S(2)}) %collective-permute-start) | collective-permute-done | bytes 4194336 | tf_op jit(solution)/shard_map/ppermute | solution.py:16
  117.9 5.9 add_select_fusion.6
  123.8 1.5 collective-permute-start.1
  125.4 7.1 collective-permute-done.1
  132.5 6.0 add_select_fusion.5
  138.5 1.7 collective-permute-start.2
  140.2 90.9 %collective-permute-done.2 = f32[4096,256]{1,0:T(8,128)} collective-permute-done((f32[4096,256]{1,0:T(8,128)}, f32[4096,256]{1,0:T(8,128)}, u32[]{:S(2)}, u32[]{:S(2)}) %collective-permute-start.2) | collective-permute-done | bytes 4194336 | tf_op jit(solution)/shard_map/ppermute | solution.py:16
  231.1 6.0 add_select_fusion.4
  237.1 3.2 collective-permute-start.3
  240.3 90.0 %collective-permute-done.3 = f32[4096,256]{1,0:T(8,128)} collective-permute-done((f32[4096,256]{1,0:T(8,128)}, f32[4096,256]{1,0:T(8,128)}, u32[]{:S(2)}, u32[]{:S(2)}) %collective-permute-start.3) | collective-permute-done | bytes 4194336 | tf_op jit(solution)/shard_map/ppermute | solution.py:16
  330.3 6.0 add_select_fusion.3
  336.3 1.2 collective-permute-start.4
  337.5 89.3 %collective-permute-done.4 = f32[4096,256]{1,0:T(8,128)} collective-permute-done((f32[4096,256]{1,0:T(8,128)}, f32[4096,256]{1,0:T(8,128)}, u32[]{:S(2)}, u32[]{:S(2)}) %collective-permute-start.4) | collective-permute-done | bytes 4194336 | tf_op jit(solution)/shard_map/ppermute | solution.py:16
  426.9 6.0 add_select_fusion.2
  432.9 2.7 collective-permute-start.5
  435.6 0.0 copy-start
  435.6 88.4 %collective-permute-done.5 = f32[4096,256]{1,0:T(8,128)} collective-permute-done((f32[4096,256]{1,0:T(8,128)}, f32[4096,256]{1,0:T(8,128)}, u32[]{:S(2)}, u32[]{:S(2)}) %collective-permute-start.5) | collective-permute-done | bytes 4194336 | tf_op jit(solution)/shard_map/ppermute | solution.py:16
  524.0 6.0 add_select_fusion.1
  530.0 1.3 collective-permute-start.6
  531.3 0.0 copy-done
  531.3 0.1 copy.21
  531.5 0.1 reshape.75
  531.6 0.1 copy.20
  531.7 0.1 copy.19
  531.9 86.9 %collective-permute-done.6 = f32[4096,256]{1,0:T(8,128)} collective-permute-done((f32[4096,256]{1,0:T(8,128)}, f32[4096,256]{1,0:T(8,128)}, u32[]{:S(2)}, u32[]{:S(2)}) %collective-permute-start.6) | collective-permute-done | bytes 4194336 | tf_op jit(solution)/shard_map/ppermute | solution.py:16
  618.7 6.0 add_select_fusion
  624.8 3.8 gather_fusion
  628.5 0.1 gather.7
  628.7 0.3 select_select_fusion
  629.0 26.1 %all_to_all.5 = f32[128,4,256]{2,1,0:T(4,128)S(1)} all-to-all(f32[128,4,256]{2,1,0:T(4,128)S(1)} %select_select_fusion), channel_id=1, replica_groups=mesh['rows'=64,'sub'=2] {'rows','sub'}, dimensions={0} | all-to-all | bytes 1048576 | tf_op jit(solution)/shard_map/all_to_all | solution.py:63
  655.2 1.7 convolution_bitcast_fusion
  656.9 0.0 all-reduce.3.cloned.1.call-update
  656.9 1.0 reshape.72
  657.9 137.5 %all-reduce.3.cloned.1.call-done = f32[256,256]{0,1:T(8,128)} async-done(((f32[256,256]{0,1:T(8,128)}), f32[256,256]{0,1:T(8,128)}) %all-reduce.3.cloned.1.call-update) | async-done | bytes 262160 | tf_op jit(solution)/shard_map/psum | solution.py:69
  795.4 1.0 broadcast_multiply_fusion.1
  796.4 0.1 copy.25
  796.5 1.0 fusion.5
  797.5 11.7 %cholesky.50 = f32[128,128]{1,0:T(8,128)S(1)} custom-call(f32[128,128]{1,0:T(8,128)S(1)} %cholesky.118), custom_call_target="Cholesky" | custom-call | tf_op jit(solution)/shard_map/jit(cholesky)/cholesky | solution.py:70
  809.3 9.8 %custom-call.11 = f32[1,128,128]{1,2,0:T(8,128)S(1)} custom-call(f32[1,128,128]{2,1,0:T(8,128)S(1)} %get-tuple-element.15), custom_call_target="InvertDiagBlocksLowerTriangular" | custom-call | tf_op jit(solution)/shard_map/jit(cholesky)/cholesky | solution.py:70
  819.1 0.2 constant_dynamic-update-slice_fusion.1
  819.3 0.3 convolution_subtract_fusion
  819.6 11.7 %cholesky.105 = f32[128,128]{1,0:T(8,128)S(1)} custom-call(f32[128,128]{1,0:T(8,128)S(1)} %convolution_subtract_fusion), custom_call_target="Cholesky" | custom-call | tf_op jit(solution)/shard_map/jit(cholesky)/cholesky | solution.py:70
  831.3 0.7 compare_reduce_fusion
  833.3 0.8 copy.26
  (8 shorter events, 0.1 us)
Async XLA Ops:
  7.2 788.2 %all-reduce.3.cloned.1.call-start = ((), (), s32[]{:S(2)}) async-start(), calls=%async_computation.1 | async-start | bytes 524288 | tf_op jit(solution)/shard_map/psum | solution.py:69
  23.9 94.0 %collective-permute-start = (f32[4096,256]{1,0:T(8,128)}, f32[4096,256]{1,0:T(8,128)}, u32[]{:S(2)}, u32[]{:S(2)}) collective-permute-start(f32[4096,256]{1,0:T(8,128)} %bitcast.3), channel_id=1, source_target_pairs={{0,1},{1,0},{2,3},{3,2},{4,5},{5,4},{6,7},{7,6},{8,9},{9,8},{10,11... | collective-permute-start | bytes 12582920 | tf_op jit(solution)/shard_map/ppermute | solution.py:16
  123.8 8.6 %collective-permute-start.1 = (f32[4096,256]{1,0:T(8,128)}, f32[4096,256]{1,0:T(8,128)}, u32[]{:S(2)}, u32[]{:S(2)}) collective-permute-start(f32[4096,256]{1,0:T(8,128)} %add_select_fusion.6), channel_id=1, source_target_pairs={{0,2},{2,0},{4,6},{6,4},{8,10},{10,8},{12,14},{14,12},{16,18},{18,... | collective-permute-start | bytes 12582920 | tf_op jit(solution)/shard_map/ppermute | solution.py:16
  138.5 92.6 %collective-permute-start.2 = (f32[4096,256]{1,0:T(8,128)}, f32[4096,256]{1,0:T(8,128)}, u32[]{:S(2)}, u32[]{:S(2)}) collective-permute-start(f32[4096,256]{1,0:T(8,128)} %add_select_fusion.5), channel_id=1, source_target_pairs={{0,4},{4,0},{2,6},{6,2},{8,12},{12,8},{10,14},{14,10},{16,20},{20,... | collective-permute-start | bytes 12582920 | tf_op jit(solution)/shard_map/ppermute | solution.py:16
  237.1 93.2 %collective-permute-start.3 = (f32[4096,256]{1,0:T(8,128)}, f32[4096,256]{1,0:T(8,128)}, u32[]{:S(2)}, u32[]{:S(2)}) collective-permute-start(f32[4096,256]{1,0:T(8,128)} %add_select_fusion.4), channel_id=1, source_target_pairs={{0,8},{8,0},{2,10},{10,2},{4,12},{12,4},{6,14},{14,6},{16,24},{24,... | collective-permute-start | bytes 12582920 | tf_op jit(solution)/shard_map/ppermute | solution.py:16
  336.3 90.6 %collective-permute-start.4 = (f32[4096,256]{1,0:T(8,128)}, f32[4096,256]{1,0:T(8,128)}, u32[]{:S(2)}, u32[]{:S(2)}) collective-permute-start(f32[4096,256]{1,0:T(8,128)} %add_select_fusion.3), channel_id=1, source_target_pairs={{0,16},{16,0},{2,18},{18,2},{4,20},{20,4},{6,22},{22,6},{8,24},{24... | collective-permute-start | bytes 12582920 | tf_op jit(solution)/shard_map/ppermute | solution.py:16
  432.9 91.1 %collective-permute-start.5 = (f32[4096,256]{1,0:T(8,128)}, f32[4096,256]{1,0:T(8,128)}, u32[]{:S(2)}, u32[]{:S(2)}) collective-permute-start(f32[4096,256]{1,0:T(8,128)} %add_select_fusion.2), channel_id=1, source_target_pairs={{0,32},{32,0},{2,34},{34,2},{4,36},{36,4},{6,38},{38,6},{8,40},{40... | collective-permute-start | bytes 12582920 | tf_op jit(solution)/shard_map/ppermute | solution.py:16
  435.6 95.7 %copy-start = (s32[1,128,4]{1,2,0:T(4,128)S(1)}, s32[1,128,4]{1,2,0:T(4,128)}, u32[]{:S(2)}) copy-start(s32[1,128,4]{1,2,0:T(4,128)} %param.5) | copy-start | bytes 6148
  530.0 88.7 %collective-permute-start.6 = (f32[4096,256]{1,0:T(8,128)}, f32[4096,256]{1,0:T(8,128)}, u32[]{:S(2)}, u32[]{:S(2)}) collective-permute-start(f32[4096,256]{1,0:T(8,128)} %add_select_fusion.1), channel_id=1, source_target_pairs={{0,64},{64,0},{2,66},{66,2},{4,68},{68,4},{6,70},{70,6},{8,72},{72... | collective-permute-start | bytes 12582920 | tf_op jit(solution)/shard_map/ppermute | solution.py:16
Sparse Core Ops, SparseCore 0:
  657.0 138.3 all-reduce.2
where the time goes:
time: 841 us
  waiting for transfers between devices  680 us (81%)
  other arithmetic  81.7 us (10%)
  blocking collectives  26.1 us (3%)
  matrix products  15.5 us (2%)
  starting transfers between devices  15.4 us (2%)
  between operations  15.4 us (2%)
    ppermute x7, waiting for transfers between devices, from_partner(): return lax.ppermute(block, axis, route)  543 us
    psum x1, waiting for transfers between devices, on_device(): gram = lax.psum(gram_part, ('rows', 'sub')) / expected  137 us
    select_n x7, other arithmetic, on_device(): values = jnp.where(upper == 1, partner - values, partner + values)  42 us
    another operation x6, other arithmetic, on_device(): factor = jnp.linalg.cholesky(gram).T  34 us
    all_to_all x1, blocking collectives, on_device(): lax.all_to_all(outgoing, ('rows', 'sub'), split_axis=0, concat_axis=0, ti...  26.1 us
  transfers between devices with their start and end apart: 8, of which 8 were waited for; matrix products, arithmetic and copies ran while one was open for 0% of the time, Pallas kernels for 0%

commit v1 on v0

v1 whole, which is shorter than its diff:
```python
import math

import jax
import jax.numpy as jnp
import numpy as np
from jax import lax
from jax.experimental import pallas as pl
from jax.experimental.pallas import tpu as pltpu
from jax.sharding import PartitionSpec as P

AXES = ("rows", "sub")
BLOCK = 256


def sylvester(order):
    matrix = np.ones((1, 1), np.float32)
    while matrix.shape[0] < order:
        matrix = np.block([[matrix, matrix], [matrix, -matrix]])
    return matrix


def butterflies(parts):
    count = len(parts)
    stride = 1
    while stride < count:
        for low in range(count):
            if low & stride == 0:
                first, second = parts[low], parts[low | stride]
                parts[low], parts[low | stride] = first + second, first - second
        stride *= 2
    return parts


def local_kernel(scale, matrix_ref, signs_ref, hadamard_ref, out_ref, held):
    step = pl.program_id(0)
    blocks = held.shape[0]
    values = matrix_ref[...]
    flips = (2 * signs_ref[0] - 1).astype(jnp.float32)
    signed = (hadamard_ref[...].astype(jnp.float32) * flips).astype(jnp.bfloat16)
    high = values.astype(jnp.bfloat16)
    rest = values - high.astype(jnp.float32)
    middle = rest.astype(jnp.bfloat16)
    low = (rest - middle.astype(jnp.float32)).astype(jnp.bfloat16)
    total = jnp.dot(signed, low, preferred_element_type=jnp.float32)
    total += jnp.dot(signed, middle, preferred_element_type=jnp.float32)
    total += jnp.dot(signed, high, preferred_element_type=jnp.float32)
    held[step] = total * scale

    @pl.when(step == blocks - 1)
    def _():
        rows, width = held.shape[1], held.shape[2]

        def body(tile, carry):
            at = pl.multiple_of(tile * 8, 8)
            for column in range(0, width, 128):
                parts = [held[b, pl.ds(at, 8), column:column + 128] for b in range(blocks)]
                parts = butterflies(parts)
                for b in range(blocks):
                    out_ref[b, pl.ds(at, 8), column:column + 128] = parts[b]
            return carry

        lax.fori_loop(0, rows // 8, body, 0)


def local_mix(matrix_rows, signs, scale):
    length, width = matrix_rows.shape
    blocks = length // BLOCK
    hadamard = jnp.asarray(sylvester(BLOCK), jnp.bfloat16)
    out = pl.pallas_call(
        lambda *refs: local_kernel(scale, *refs),
        grid=(blocks,),
        out_shape=jax.ShapeDtypeStruct((blocks, BLOCK, width), jnp.float32),
        in_specs=[
            pl.BlockSpec((BLOCK, width), lambda b: (b, 0)),
            pl.BlockSpec((1, 1, BLOCK), lambda b: (b, 0, 0)),
            pl.BlockSpec((BLOCK, BLOCK), lambda b: (0, 0)),
        ],
        out_specs=pl.BlockSpec((blocks, BLOCK, width), lambda b: (0, 0, 0)),
        scratch_shapes=[pltpu.VMEM((blocks, BLOCK, width), jnp.float32)],
        compiler_params=pltpu.CompilerParams(vmem_limit_bytes=32 * 2**20),
        name="local_mix",
    )(matrix_rows, signs.reshape(blocks, 1, BLOCK), hadamard)
    return out


def across_kernel(in_ref, out_ref):
    count = in_ref.shape[0]
    inner = 8
    outer = count // inner
    for group in range(inner):
        parts = butterflies([in_ref[b * inner + group] for b in range(outer)])
        for b in range(outer):
            out_ref[b * inner + group] = parts[b]
    for group in range(outer):
        parts = butterflies([out_ref[group * inner + b] for b in range(inner)])
        for b in range(inner):
            out_ref[group * inner + b] = parts[b]


def across_mix(values):
    count, rows, width = values.shape
    spec = pl.BlockSpec((count, 8, 128), lambda r, c: (0, r, c))
    return pl.pallas_call(
        across_kernel,
        grid=(rows // 8, width // 128),
        out_shape=jax.ShapeDtypeStruct(values.shape, jnp.float32),
        in_specs=[spec],
        out_specs=spec,
        compiler_params=pltpu.CompilerParams(vmem_limit_bytes=32 * 2**20),
        name="across_mix",
    )(values)


def exchange(block):
    return lax.all_to_all(block, AXES, split_axis=0, concat_axis=0, tiled=True)


def on_device(matrix_rows, signs, picks):
    length, width = matrix_rows.shape
    owners = lax.axis_size("rows") * lax.axis_size("sub")
    share = length // owners
    scale = 1.0 / math.sqrt(length * owners)
    slots = picks[0]
    flat_picks = slots.reshape(-1)

    holder = (flat_picks // share)[:, None] == lax.broadcasted_iota(jnp.int32, (1, owners), 1)
    place = (flat_picks % share)[:, None] == lax.broadcasted_iota(jnp.int32, (1, share), 1)
    holder = holder & (flat_picks >= 0)[:, None]
    times = lax.dot_general(
        holder.astype(jnp.bfloat16), place.astype(jnp.bfloat16), (((0,), (0,)), ((), ())),
        preferred_element_type=jnp.float32,
    )
    times = exchange(times[:, None, :]).reshape(owners * share, 1)

    local = local_mix(matrix_rows, signs, scale)
    gathered = exchange(local.reshape(owners, share, width))
    whole = across_mix(gathered)
    values = exchange(whole).reshape(length, width)

    flat = whole.reshape(owners * share, width)
    gram = lax.dot_general(
        flat * times, flat, (((0,), (0,)), ((), ())),
        precision=lax.Precision.HIGHEST, preferred_element_type=jnp.float32,
    )
    gram = jnp.sum(exchange(gram.reshape(owners, width // owners, width)), axis=0)
    gram = exchange(jnp.broadcast_to(gram[None], (owners,) + gram.shape)).reshape(width, width)
    expected = owners * owners * slots.shape[1] / 2.0
    factor = jnp.linalg.cholesky(gram / expected).T

    taken = jnp.take(values, jnp.maximum(flat_picks, 0), axis=0)
    taken = jnp.where((flat_picks >= 0)[:, None], taken, jnp.float32(0.0))
    panel = exchange(taken.reshape(slots.shape[0], slots.shape[1], width)).reshape(-1, width)
    return (values, panel, factor)


def solution(mesh):
    placed = (P(AXES, None), P(AXES), P(AXES, None, None))
    return jax.shard_map(
        on_device,
        mesh=mesh,
        in_specs=placed,
        out_specs=(P(AXES, None), P(AXES, None), P()),
        check_vma=False,
    )
```

time: 841 us -> 244 us (0.29)
  waiting for transfers between devices: 680 us -> 81.9 us
  other arithmetic: 81.7 us -> 41 us
  local copies, waits for them, and re-layouts: 6.37 us -> 32.1 us
  starting transfers between devices: 15.4 us -> 32.5 us
  between operations: 15.4 us -> 2.17 us
  Pallas kernels: 0 us -> 11.2 us
    ppermute x7 -> x0, waiting for transfers between devices: 543 us -> none  [from_partner(): return lax.ppermute(block, axis, route)]
    psum x1 -> x0, waiting for transfers between devices: 137 us -> none  [on_device(): gram = lax.psum(gram_part, ('rows', 'sub')) / expected]
    all_to_all x0 -> x4, waiting for transfers between devices: none -> 81.9 us  [exchange(): return lax.all_to_all(block, AXES, split_axis=0, concat_axis=0, tiled=True)]
    select_n x7 -> x1, other arithmetic: 42 us -> 0.01 us  [on_device(): flat_picks // share]
    all_to_all x0 -> x4, starting transfers between devices: none -> 32.5 us  [exchange(): return lax.all_to_all(block, AXES, split_axis=0, concat_axis=0, tiled=True)]
    ppermute x7 -> x0, starting transfers between devices: 15.4 us -> none  [from_partner(): return lax.ppermute(block, axis, route)]
    unnamed x3 -> x15, local copies, waits for them, and re-layouts: 0.84 us -> 13.9 us
    pallas_call x0 -> x2, Pallas kernels: none -> 11.2 us  [the longest x1 5.79 us: local_mix(): pl.pallas_call(lambda *refs: local_kernel(scale, *refs), grid=(blocks,),...]
  transfers between devices with their start and end apart: 8 -> 4, of which waited for: 8 -> 3; matrix products, arithmetic and copies ran while one was open for 0% -> 15% of each run, Pallas kernels for 0% -> 2%
where the time goes in v1:
time: 244 us; the launch traced here: 243 us
  waiting for transfers between devices  81.9 us (34%)
  other arithmetic  41 us (17%)
  starting transfers between devices  32.5 us (13%)
  local copies, waits for them, and re-layouts  32.1 us (13%)
  blocking collectives  31.6 us (13%)
  Pallas kernels  11.2 us (5%)
  matrix products  10.9 us (4%)
    all_to_all x4, waiting for transfers between devices, exchange(): return lax.all_to_all(block, AXES, split_axis=0, concat_axis=0, tiled=True)  81.9 us
    another operation x6, other arithmetic, on_device(): factor = jnp.linalg.cholesky(gram / expected).T  33.9 us
    all_to_all x4, starting transfers between devices, exchange(): return lax.all_to_all(block, AXES, split_axis=0, concat_axis=0, tiled=True)  32.5 us
    all_to_all x2, blocking collectives, exchange(): return lax.all_to_all(block, AXES, split_axis=0, concat_axis=0, tiled=True)  31.6 us
    unnamed x15, local copies, waits for them, and re-layouts  13.9 us
    dot_general x1, matrix products, on_device(): lax.dot_general(flat * times, flat, (((0,), (0,)), ((), ())), precision=l...  9.31 us
    dot_general x2, local copies, waits for them, and re-layouts, on_device(): lax.dot_general(flat * times, flat, (((0,), (0,)), ((), ())), precision=l...  6.02 us
    pallas_call x1, Pallas kernels, local_mix(): pl.pallas_call(lambda *refs: local_kernel(scale, *refs), grid=(blocks,),...  5.79 us
  transfers between devices with their start and end apart: 4, of which 3 were waited for; matrix products, arithmetic and copies ran while one was open for 15% of the time, Pallas kernels for 2%

profile of v1, /device:TPU:1, one launch (start us, length us, event | category | flops | bytes accessed | tf_op | source)
XLA Modules:
  0.0 243.3 jit_solution(9505089475288029938)
XLA Ops:
  0.6 0.8 copy.23
  1.4 0.1 reshape_squeeze.3
  1.6 1.1 fusion.4
  2.7 11.5 %all-to-all-start.3 = ((f32[128,1,32]{2,1,0:T(1,128)}), f32[128,1,32]{2,1,0:T(1,128)S(1)}, u32[]{:S(2)}, u32[]{:S(2)}) async-start(f32[128,1,32]{2,1,0:T(1,128)} %bitcast.14), calls=%async_computation.3 | async-start | bytes 131072 | tf_op jit(solution)/shard_map/all_to_all | solution.py:115
  14.2 0.0 copy-start.2
  14.2 2.2 copy-done.2
  16.4 0.0 copy-start.3
  16.4 0.9 copy-done.3
  17.3 0.0 copy-start.4
  17.3 0.7 copy-done.4
  18.0 5.8 %local_mix.1 = f32[16,256,256]{2,1,0:T(8,128)S(1)} custom-call(f32[4096,256]{1,0:T(8,128)S(1)} %copy-done.2, s32[16,1,256]{2,1,0:T(1,128)S(1)} %bitcast.33, bf16[256,256]{1,0:T(8,128)(2,1)S(1)} %copy-done.3), custom_call_target="tpu_custom_call" | custom-call | tf_op jit(solution)/shard_map/local_mix/pallas_call | solution.py:69
  23.8 0.0 copy-start.1
  23.8 2.0 copy-done.1
  25.8 0.0 all-to-all-done.3
  25.8 10.2 %all-to-all-start = ((f32[128,32,256]{2,1,0:T(8,128)}), f32[128,32,256]{2,1,0:T(8,128)}, u32[]{:S(2)}, u32[]{:S(2)}) async-start(f32[128,32,256]{2,1,0:T(8,128)} %bitcast.32), calls=%async_computation | async-start | bytes 8388608 | tf_op jit(solution)/shard_map/all_to_all | solution.py:115
  36.0 0.5 broadcast.204
  36.5 0.8 reduce.15
  37.4 0.1 mul.10
  37.4 52.4 %all-to-all-done.in_ref = f32[128,32,256]{2,1,0:T(8,128)} async-done(((f32[128,32,256]{2,1,0:T(8,128)}), f32[128,32,256]{2,1,0:T(8,128)}, u32[]{:S(2)}, u32[]{:S(2)}) %all-to-all-start) | async-done | bytes 4194336 | tf_op jit(solution)/shard_map/all_to_all | solution.py:115
  89.8 5.4 %across_mix.1 = f32[128,32,256]{2,1,0:T(8,128)S(1)} custom-call(f32[128,32,256]{2,1,0:T(8,128)} %all-to-all-done.in_ref), custom_call_target="tpu_custom_call" | custom-call | tf_op jit(solution)/shard_map/across_mix/pallas_call | solution.py:103
  95.2 0.0 copy-start
  95.2 2.0 copy-done
  97.2 5.7 %copy.25 = f32[4096,256]{0,1:T(8,128)} copy(f32[4096,256]{1,0:T(8,128)} %bitcast.30) | data formatting | bytes 8388608 | tf_op jit(solution)/shard_map/reshape | solution.py:140
  102.9 4.8 %multiply_bitcast_fusion = f32[256,4096]{1,0:T(8,128)} fusion(f32[4096,256]{0,1:T(8,128)} %copy.25, f32[4096]{0:T(1024)S(1)} %mul.10), kind=kLoop, calls=%fused_computation.3 | loop fusion | flops 1048576 | bytes 8404992 | tf_op jit(solution)/shard_map/dot_general | solution.py:141
  107.7 5.8 %dot_general.12 = f32[128,2,4096]{2,1,0:T(2,128)} reshape(f32[256,4096]{1,0:T(8,128)} %multiply_bitcast_fusion) | data formatting | bytes 8388608 | tf_op jit(solution)/shard_map/dot_general | solution.py:141
  113.5 9.3 %fusion = f32[128,2,256]{2,0,1:T(8,128)S(1)} fusion(f32[4096,256,1]{1,0,2:T(8,128)} %bitcast.31, f32[128,2,4096]{2,1,0:T(2,128)} %dot_general.12), kind=kOutput, calls=%fused_computation.1 | convolution fusion | flops 3221225472 | bytes 8650752 | tf_op jit(solution)/shard_map/dot_general | solution.py:141
  122.8 0.2 copy.27
  123.0 16.3 %all_to_all.30 = f32[128,2,256]{2,1,0:T(2,128)S(1)} all-to-all(f32[128,2,256]{2,1,0:T(2,128)S(1)} %copy.27), channel_id=1, replica_groups=mesh['rows'=64,'sub'=2] {'rows','sub'}, dimensions={0} | all-to-all | bytes 524288 | tf_op jit(solution)/shard_map/all_to_all | solution.py:115
  139.3 0.1 reduce_sum.9
  139.4 0.1 broadcast_in_dim.42
  139.5 15.3 %all_to_all.31 = f32[128,2,256]{2,1,0:T(2,128)S(1)} all-to-all(f32[128,2,256]{2,1,0:T(2,128)S(1)} %broadcast_in_dim.42), channel_id=1, replica_groups=mesh['rows'=64,'sub'=2] {'rows','sub'}, dimensions={0} | all-to-all | bytes 524288 | tf_op jit(solution)/shard_map/all_to_all | solution.py:115
  154.9 0.0 copy-start.5
  154.9 5.3 %all-to-all-start.1 = ((f32[128,32,256]{2,1,0:T(8,128)}), f32[128,32,256]{2,1,0:T(8,128)}, u32[]{:S(2)}, u32[]{:S(2)}) async-start(f32[128,32,256]{2,1,0:T(8,128)} %copy-done), calls=%async_computation.1 | async-start | bytes 8388608 | tf_op jit(solution)/shard_map/all_to_all | solution.py:115
  160.2 0.0 copy-done.5
  160.2 0.1 copy.22
  160.3 0.1 reshape.140
  160.5 0.1 copy.20
  160.6 0.1 copy.21
  160.8 0.1 broadcast_multiply_fusion
  160.9 0.2 div.34
  161.1 0.1 copy.28
  161.3 11.7 %cholesky.50 = f32[128,128]{1,0:T(8,128)S(1)} custom-call(f32[128,128]{1,0:T(8,128)S(1)} %cholesky.118), custom_call_target="Cholesky" | custom-call | tf_op jit(solution)/shard_map/jit(cholesky)/cholesky | solution.py:148
  173.0 9.8 %custom-call.11 = f32[1,128,128]{1,2,0:T(8,128)S(1)} custom-call(f32[1,128,128]{2,1,0:T(8,128)S(1)} %get-tuple-element.15), custom_call_target="InvertDiagBlocksLowerTriangular" | custom-call | tf_op jit(solution)/shard_map/jit(cholesky)/cholesky | solution.py:148
  182.8 0.2 constant_dynamic-update-slice_fusion.1
  183.1 0.3 convolution_subtract_fusion
  183.3 11.7 %cholesky.105 = f32[128,128]{1,0:T(8,128)S(1)} custom-call(f32[128,128]{1,0:T(8,128)S(1)} %convolution_subtract_fusion), custom_call_target="Cholesky" | custom-call | tf_op jit(solution)/shard_map/jit(cholesky)/cholesky | solution.py:148
  195.0 19.1 %all-to-all-done.1 = f32[128,32,256]{2,1,0:T(8,128)} async-done(((f32[128,32,256]{2,1,0:T(8,128)}), f32[128,32,256]{2,1,0:T(8,128)}, u32[]{:S(2)}, u32[]{:S(2)}) %all-to-all-start.1) | async-done | bytes 4194336 | tf_op jit(solution)/shard_map/all_to_all | solution.py:115
  214.2 3.8 %gather_fusion = f32[512,256]{1,0:T(8,128)S(1)} fusion(f32[4096,256]{1,0:T(8,128)} %bitcast.2, s32[1024]{0:T(1024)S(1)} %pad_clamp_fusion), kind=kCustom, calls=%fused_computation | custom fusion | bytes 1050624 | tf_op jit(solution)/shard_map/jit(_take)/gather | solution.py:150
  217.9 0.1 gather.7
  218.1 1.1 select_select_fusion
  219.2 5.5 %all-to-all-start.2 = ((f32[128,4,256]{2,1,0:T(4,128)}), f32[128,4,256]{2,1,0:T(4,128)S(1)}, u32[]{:S(2)}, u32[]{:S(2)}) async-start(f32[128,4,256]{2,1,0:T(4,128)} %select_select_fusion), calls=%async_computation.2 | async-start | bytes 1048576 | tf_op jit(solution)/shard_map/all_to_all | solution.py:115
  224.7 0.6 compare_reduce_fusion
  226.7 0.8 copy.29
  227.5 10.4 %all-to-all-done.2 = f32[128,4,256]{2,1,0:T(4,128)S(1)} async-done(((f32[128,4,256]{2,1,0:T(4,128)}), f32[128,4,256]{2,1,0:T(4,128)S(1)}, u32[]{:S(2)}, u32[]{:S(2)}) %all-to-all-start.2) | async-done | bytes 524320 | tf_op jit(solution)/shard_map/all_to_all | solution.py:115
  237.9 1.0 reshape.136
  238.9 4.5 %copy.35 = f32[4096,256]{1,0:T(8,128)} copy(f32[4096,256]{1,0:T(8,128)} %bitcast.2) | data formatting | bytes 8388608
  (11 shorter events, 0.2 us)
Async XLA Ops:
  2.7 23.1 %all-to-all-start.3 = ((f32[128,1,32]{2,1,0:T(1,128)}), f32[128,1,32]{2,1,0:T(1,128)S(1)}, u32[]{:S(2)}, u32[]{:S(2)}) async-start(f32[128,1,32]{2,1,0:T(1,128)} %bitcast.14), calls=%async_computation.3 | async-start | bytes 131072 | tf_op jit(solution)/shard_map/all_to_all | solution.py:115
  14.2 2.2 copy-start.2
  16.4 0.9 copy-start.3
  17.3 0.7 copy-start.4
  23.8 2.0 copy-start.1
  25.8 64.0 %all-to-all-start = ((f32[128,32,256]{2,1,0:T(8,128)}), f32[128,32,256]{2,1,0:T(8,128)}, u32[]{:S(2)}, u32[]{:S(2)}) async-start(f32[128,32,256]{2,1,0:T(8,128)} %bitcast.32), calls=%async_computation | async-start | bytes 8388608 | tf_op jit(solution)/shard_map/all_to_all | solution.py:115
  95.2 2.0 copy-start
  154.9 5.4 %copy-start.5 = (s32[1,128,4]{1,2,0:T(4,128)S(1)}, s32[1,128,4]{1,2,0:T(4,128)}, u32[]{:S(2)}) copy-start(s32[1,128,4]{1,2,0:T(4,128)} %param.6) | copy-start | bytes 6148
  154.9 59.3 %all-to-all-start.1 = ((f32[128,32,256]{2,1,0:T(8,128)}), f32[128,32,256]{2,1,0:T(8,128)}, u32[]{:S(2)}, u32[]{:S(2)}) async-start(f32[128,32,256]{2,1,0:T(8,128)} %copy-done), calls=%async_computation.1 | async-start | bytes 8388608 | tf_op jit(solution)/shard_map/all_to_all | solution.py:115
  219.2 18.7 %all-to-all-start.2 = ((f32[128,4,256]{2,1,0:T(4,128)}), f32[128,4,256]{2,1,0:T(4,128)S(1)}, u32[]{:S(2)}, u32[]{:S(2)}) async-start(f32[128,4,256]{2,1,0:T(4,128)} %select_select_fusion), calls=%async_computation.2 | async-start | bytes 1048576 | tf_op jit(solution)/shard_map/all_to_all | solution.py:115

commit v2 on v1

v2 whole, which is shorter than its diff:
```python
import math

import jax
import jax.numpy as jnp
from jax import lax
from jax.experimental import pallas as pl
from jax.experimental.pallas import tpu as pltpu
from jax.sharding import PartitionSpec as P

AXES = ("rows", "sub")
TILE = 8
RADIX = 8
SUPER = 32
VMEM = 40 * 2**20
LARGE = 57 * 2**20


def butterflies(parts):
    count = len(parts)
    stride = 1
    while stride < count:
        for low in range(count):
            if low & stride == 0:
                first, second = parts[low], parts[low | stride]
                parts[low], parts[low | stride] = first + second, first - second
        stride *= 2
    return parts


def whole(space=pltpu.VMEM):
    return pl.BlockSpec(memory_space=space)


def local_kernel(scale, matrix_ref, signs_ref, out_ref, came, first, second, third, flips, signs_held, sems):
    halves, length, _ = came.shape
    share = out_ref.shape[1]
    size = length // RADIX
    group = TILE * RADIX
    loads = [
        [
            pltpu.make_async_copy(
                matrix_ref.at[pl.ds(c * size, size), h * 128:h * 128 + 128],
                came.at[h, pl.ds(c * size, size)],
                sems.at[c * halves + h],
            )
            for h in range(halves)
        ]
        for c in range(RADIX)
    ]
    signs_load = pltpu.make_async_copy(signs_ref, signs_held, sems.at[RADIX * halves])
    signs_load.start()
    for pair in loads:
        for load in pair:
            load.start()

    row = lax.broadcasted_iota(jnp.int32, (128, 128), 0)
    column = lax.broadcasted_iota(jnp.int32, (128, 128), 1)
    chosen = (row // 64 * 64 + row % 8 * 8 + row // 8 % 8 == column).astype(jnp.float32)
    ones = jnp.ones((128, 128), jnp.bfloat16)
    signs_load.wait()

    def flip(line, carry):
        signs = (2 * signs_held[pl.ds(line, 1), :] - 1).astype(jnp.float32)
        flips[pl.ds(pl.multiple_of(line * 128, 128), 128), :] = scale * jnp.dot(
            (chosen * signs).astype(jnp.bfloat16), ones, preferred_element_type=jnp.float32
        )
        return carry

    lax.fori_loop(0, length // 128, flip, 0, unroll=4)

    for c in range(RADIX):
        for load in loads[c]:
            load.wait()

        def inner(g, carry):
            base = pl.multiple_of(c * size + g * group, group)
            signs = [flips[pl.ds(base + TILE * s, TILE), :] for s in range(TILE)]
            for h in range(halves):
                parts = [came[h, pl.ds(base + s, RADIX, stride=TILE), :] * signs[s] for s in range(TILE)]
                parts = butterflies(parts)
                for s in range(TILE):
                    first[h, pl.ds(base + s, RADIX, stride=TILE), :] = parts[s]
            for h in range(halves):
                parts = butterflies([first[h, pl.ds(base + TILE * t, TILE), :] for t in range(RADIX)])
                for t in range(RADIX):
                    second[h, pl.ds(base + TILE * t, TILE), :] = parts[t]
            return carry

        lax.fori_loop(0, size // group, inner, 0, unroll=2)

        def outer(t, carry):
            base = pl.multiple_of(c * size + t * TILE, TILE)
            for h in range(halves):
                parts = butterflies([second[h, pl.ds(base + group * g, TILE), :] for g in range(size // group)])
                for g in range(size // group):
                    third[h, pl.ds(base + group * g, TILE), :] = parts[g]
            return carry

        lax.fori_loop(0, group // TILE, outer, 0, unroll=2)

    def last(q, carry):
        for t in range(share // TILE):
            for h in range(halves):
                at = pl.multiple_of(q * share, share) + t * TILE
                parts = butterflies([third[h, pl.ds(c * size + at, TILE), :] for c in range(RADIX)])
                for c in range(RADIX):
                    out_ref[c * (size // share) + q, t * TILE:(t + 1) * TILE, h * 128:h * 128 + 128] = parts[c]
        return carry

    lax.fori_loop(0, size // share, last, 0)


def local_mix(matrix_rows, signs, scale, owners):
    length, width = matrix_rows.shape
    halves = width // 128
    return pl.pallas_call(
        lambda *refs: local_kernel(scale, *refs),
        out_shape=jax.ShapeDtypeStruct((owners, length // owners, width), jnp.float32),
        in_specs=[whole(pltpu.HBM)] * 2,
        out_specs=whole(),
        scratch_shapes=[pltpu.VMEM((halves, length, 128), jnp.float32)] * 4
        + [
            pltpu.VMEM((length, 128), jnp.float32),
            pltpu.VMEM((length // 128, 128), jnp.int32),
            pltpu.SemaphoreType.DMA((RADIX * halves + 1,)),
        ],
        compiler_params=pltpu.CompilerParams(vmem_limit_bytes=LARGE),
        name="local_mix",
    )(matrix_rows, signs.reshape(length // 128, 128))


def across_kernel(in_ref, out_ref, held):
    count, rows, width = in_ref.shape
    inner = 8
    outer = count // inner

    def body(tile, carry):
        at = pl.multiple_of(tile * 8, 8)
        for half in range(width // 128):
            columns = slice(half * 128, half * 128 + 128)
            for group in range(inner):
                parts = butterflies([in_ref[b * inner + group, pl.ds(at, 8), columns] for b in range(outer)])
                for b in range(outer):
                    held[b * inner + group] = parts[b]
            for group in range(outer):
                parts = butterflies([held[group * inner + b] for b in range(inner)])
                for b in range(inner):
                    out_ref[group * inner + b, half, pl.ds(at, 8), :] = parts[b]
        return carry

    lax.fori_loop(0, rows // 8, body, 0)


def across_mix(values):
    count, rows, width = values.shape
    return pl.pallas_call(
        across_kernel,
        out_shape=jax.ShapeDtypeStruct((count, width // 128, rows, 128), jnp.float32),
        in_specs=[whole()],
        out_specs=whole(),
        scratch_shapes=[pltpu.VMEM((count, 8, 128), jnp.float32)],
        compiler_params=pltpu.CompilerParams(vmem_limit_bytes=VMEM),
        name="across_mix",
    )(values)


def pick_kernel(picks_ref, values_ref, mixed_ref, out_ref, taken, sems):
    halves, rows = values_ref.shape[1], values_ref.shape[2]
    tiles, _, slots, _ = taken.shape
    each = out_ref.shape[2]
    copies = [
        pltpu.make_async_copy(
            values_ref.at[:, half], mixed_ref.at[:, :, half * 128:half * 128 + 128], sems.at[half]
        )
        for half in range(halves)
    ]
    for copy in copies:
        copy.start()

    def body(tile, carry):
        for slot in range(slots):
            pick = picks_ref[slot % each, tile * (slots // each) + slot // each]
            row = jnp.maximum(pick, 0)
            for half in range(halves):
                part = values_ref[row // rows, half, pl.ds(row % rows, 1), :]
                taken[tile, half, slot:slot + 1, :] = jnp.where(pick >= 0, part, 0.0)
        for half in range(halves):
            for place in range(slots // each):
                out_ref[tile * (slots // each) + place, half] = (
                    taken[tile, half, place * each:(place + 1) * each, :]
                )
        return carry

    lax.fori_loop(0, tiles, body, 0, unroll=2)
    panel = jnp.concatenate([taken[:, half].reshape(-1, 128) for half in range(halves)], axis=1)
    gram = lax.dot_general(
        panel, panel, (((0,), (0,)), ((), ())),
        precision=lax.Precision.HIGHEST, preferred_element_type=jnp.float32,
    )
    each = gram.shape[0] // out_ref.shape[0]
    for owner in range(out_ref.shape[0]):
        for half in range(halves):
            out_ref[owner, halves, half * each:(half + 1) * each, :] = (
                gram[owner * each:(owner + 1) * each, half * 128:half * 128 + 128]
            )
    for copy in copies:
        copy.wait()


def pick_rows(values, picks):
    count, halves, rows, _ = values.shape
    slots, owners = picks.shape
    return pl.pallas_call(
        pick_kernel,
        out_shape=(
            jax.ShapeDtypeStruct((count, rows, halves * 128), jnp.float32),
            jax.ShapeDtypeStruct((owners, halves + 1, slots, 128), jnp.float32),
        ),
        in_specs=[whole(pltpu.SMEM), whole()],
        out_specs=(whole(pltpu.HBM), whole()),
        scratch_shapes=[
            pltpu.VMEM((slots * owners // TILE, halves, TILE, 128), jnp.float32),
            pltpu.SemaphoreType.DMA((halves,)),
        ],
        compiler_params=pltpu.CompilerParams(vmem_limit_bytes=VMEM),
        name="pick_rows",
    )(picks, values)


def sum_kernel(received_ref, out_ref):
    sources, last = received_ref.shape[0], received_ref.shape[1] - 1
    total = jnp.sum(received_ref[:, last], axis=0)
    out_ref[...] = jnp.broadcast_to(total[None], out_ref.shape)


def sum_pieces(received):
    sources, _, rows, width = received.shape
    return pl.pallas_call(
        sum_kernel,
        out_shape=jax.ShapeDtypeStruct((sources, rows, width), jnp.float32),
        in_specs=[whole()],
        out_specs=whole(),
        compiler_params=pltpu.CompilerParams(vmem_limit_bytes=VMEM),
        name="sum_pieces",
    )(received)


def panel_kernel(received_ref, panel_ref):
    sources, last, slots, _ = received_ref.shape
    for source in range(sources):
        for half in range(last - 1):
            panel_ref[source * slots:(source + 1) * slots, half * 128:half * 128 + 128] = (
                received_ref[source, half]
            )


def arrange_panel(received):
    sources, last, slots, width = received.shape
    return pl.pallas_call(
        panel_kernel,
        out_shape=jax.ShapeDtypeStruct((sources * slots, (last - 1) * width), jnp.float32),
        in_specs=[whole()],
        out_specs=whole(),
        compiler_params=pltpu.CompilerParams(vmem_limit_bytes=VMEM),
        name="arrange_panel",
    )(received)


def cholesky_kernel(expected, pieces_ref, out_ref, held):
    size = held.shape[0]
    halves = size // 128
    each = pieces_ref.shape[1] // halves
    for owner in range(pieces_ref.shape[0]):
        for half in range(halves):
            held[owner * each:(owner + 1) * each, half * 128:half * 128 + 128] = (
                pieces_ref[owner, half * each:(half + 1) * each, :] * (1.0 / expected)
            )
    place = lax.broadcasted_iota(jnp.int32, (TILE, 128), 0)
    lane = lax.broadcasted_iota(jnp.int32, (TILE, 128), 1)

    def spread_row(value, row):
        return jnp.broadcast_to(value[row:row + 1, :], (TILE, 128))

    def spread_column(value, column):
        return jnp.broadcast_to(value[:, column:column + 1], (TILE, 128))

    for base in range(0, size, SUPER):
        tiles = SUPER // TILE
        rows = [
            [held[base + t * TILE:base + (t + 1) * TILE, h * 128:h * 128 + 128] for h in range(halves)]
            for t in range(tiles)
        ]
        for t in range(tiles):
            first = base + t * TILE
            half, column = first // 128, first % 128
            edges = {
                u: [spread_column(rows[u][half], column + k) for k in range(TILE)]
                for u in range(t, tiles)
            }
            finished = list(rows[t])
            for k in range(TILE):
                pivot = spread_row(edges[t][k], k)
                inverse = 1.0 / pivot
                root = lax.rsqrt(pivot)
                root = root * (1.5 - 0.5 * pivot * root * root)
                lines = [spread_row(rows[t][h], k) for h in range(halves)]
                finished = [
                    jnp.where(place == k, lines[h] * root, finished[h]) for h in range(halves)
                ]
                lines = [line * inverse for line in lines]
                weights = [None] * TILE
                for m in range(k + 1, TILE):
                    weights[m] = spread_row(edges[t][k], m) * inverse
                for u in range(t, tiles):
                    edge = edges[u][k]
                    for m in range(k + 1, TILE):
                        edges[u][m] = edges[u][m] - edge * weights[m]
                    for h in range(halves):
                        rows[u][h] = rows[u][h] - edge * lines[h]
            rows[t] = [
                jnp.where(lane + h * 128 >= first + place, finished[h], 0.0) for h in range(halves)
            ]
            for h in range(halves):
                out_ref[first:first + TILE, h * 128:h * 128 + 128] = rows[t][h]
        after = base + SUPER
        if after < size:
            block = jnp.concatenate(
                [jnp.concatenate(rows[t], axis=1) for t in range(tiles)], axis=0
            )
            turned = block.T[after:]
            held[after:, :] -= jnp.dot(
                turned, block, precision=lax.Precision.HIGHEST, preferred_element_type=jnp.float32
            )


def upper_cholesky(pieces, expected):
    owners, rows, width = pieces.shape
    size = math.isqrt(owners * rows * width)
    return pl.pallas_call(
        lambda *refs: cholesky_kernel(expected, *refs),
        out_shape=jax.ShapeDtypeStruct((size, size), jnp.float32),
        in_specs=[whole()],
        out_specs=whole(),
        scratch_shapes=[pltpu.VMEM((size, size), jnp.float32)],
        compiler_params=pltpu.CompilerParams(vmem_limit_bytes=VMEM),
        name="upper_cholesky",
    )(pieces)


def exchange(block):
    return lax.all_to_all(block, AXES, split_axis=0, concat_axis=0, tiled=True)


def on_device(matrix_rows, signs, picks):
    length, width = matrix_rows.shape
    owners = lax.axis_size("rows") * lax.axis_size("sub")
    slots = picks.shape[2]
    scale = 1.0 / math.sqrt(length * owners)
    expected = owners * owners * slots / 2.0

    values = exchange(across_mix(exchange(local_mix(matrix_rows, signs, scale, owners))))
    mixed, taken = pick_rows(values, picks[0].T)
    received = exchange(taken)
    pieces = exchange(sum_pieces(received))
    factor = upper_cholesky(pieces, expected)
    panel = arrange_panel(received)
    return (mixed.reshape(length, width), panel, factor)


def solution(mesh):
    placed = (P(AXES, None), P(AXES), P(AXES, None, None))
    return jax.shard_map(
        on_device,
        mesh=mesh,
        in_specs=placed,
        out_specs=(P(AXES, None), P(AXES, None), P()),
        check_vma=False,
    )
```

time: 244 us -> 187 us (0.77)
  blocking collectives: 31.6 us -> 146 us
  waiting for transfers between devices: 81.9 us -> 10.1 us
  other arithmetic: 41 us -> 0 us
  local copies, waits for them, and re-layouts: 32.1 us -> 0.01 us
  starting transfers between devices: 32.5 us -> 5.36 us
  Pallas kernels: 11.2 us -> 24.7 us
  matrix products: 10.9 us -> 0 us
    all_to_all x2 -> x3, blocking collectives: 31.6 us -> 146 us  [exchange(): return lax.all_to_all(block, AXES, split_axis=0, concat_axis=0, tiled=True)]
    all_to_all x4 -> x1, waiting for transfers between devices: 81.9 us -> 10.1 us  [exchange(): return lax.all_to_all(block, AXES, split_axis=0, concat_axis=0, tiled=True)]
    another operation x6 -> x0, other arithmetic: 33.9 us -> none  [on_device(): factor = jnp.linalg.cholesky(gram / expected).T]
    all_to_all x4 -> x1, starting transfers between devices: 32.5 us -> 5.36 us  [exchange(): return lax.all_to_all(block, AXES, split_axis=0, concat_axis=0, tiled=True)]
    unnamed x15 -> x2, local copies, waits for them, and re-layouts: 13.9 us -> 0.01 us
    pallas_call x2 -> x6, Pallas kernels: 11.2 us -> 24.7 us  [the longest x1 9.42 us: upper_cholesky(): pl.pallas_call(lambda *refs: cholesky_kernel(expected, *refs), out_shape=...]
    dot_general x2 -> x0, matrix products: 10.4 us -> none  [the longest x1 9.31 us: on_device(): lax.dot_general(flat * times, flat, (((0,), (0,)), ((), ())), precision=l...]
    reshape x2 -> x0, local copies, waits for them, and re-layouts: 6.63 us -> none  [the longest x1 5.66 us: on_device(): flat = whole.reshape(owners * share, width)]
  transfers between devices with their start and end apart: 4 -> 1, of which waited for: 3 -> 1; matrix products, arithmetic and copies ran while one was open for 15% -> 0% of each run, Pallas kernels for 2% -> 0%
where the time goes in v2:
time: 187 us
  blocking collectives  146 us (78%)
  Pallas kernels  24.7 us (13%)
  waiting for transfers between devices  10.1 us (5%)
  starting transfers between devices  5.36 us (3%)
    all_to_all x3, blocking collectives, exchange(): return lax.all_to_all(block, AXES, split_axis=0, concat_axis=0, tiled=True)  146 us
    all_to_all x1, waiting for transfers between devices, exchange(): return lax.all_to_all(block, AXES, split_axis=0, concat_axis=0, tiled=True)  10.1 us
    pallas_call x1, Pallas kernels, upper_cholesky(): pl.pallas_call(lambda *refs: cholesky_kernel(expected, *refs), out_shape=...  9.42 us
    pallas_call x1, Pallas kernels, local_mix(): pl.pallas_call(lambda *refs: local_kernel(scale, *refs), out_shape=jax.Sh...  7.55 us
    all_to_all x1, starting transfers between devices, exchange(): return lax.all_to_all(block, AXES, split_axis=0, concat_axis=0, tiled=True)  5.36 us
    pallas_call x1, Pallas kernels, pick_rows(): pl.pallas_call(pick_kernel, out_shape=(jax.ShapeDtypeStruct((count, rows,...  4.27 us
  transfers between devices with their start and end apart: 1, of which 1 were waited for; matrix products, arithmetic and copies ran while one was open for 0% of the time, Pallas kernels for 0%

profile of v2, /device:TPU:1, one launch (start us, length us, event | category | flops | bytes accessed | tf_op | source)
XLA Modules:
  0.0 186.9 jit_solution(11107278709239671111)
XLA Ops:
  0.6 7.6 %local_mix.1 = f32[128,32,256]{2,1,0:T(8,128)} custom-call(f32[4096,256]{1,0:T(8,128)} %refs_0_.1, s32[32,128]{1,0:T(8,128)} %bitcast.6), custom_call_target="tpu_custom_call" | custom-call | tf_op jit(solution)/shard_map/local_mix/pallas_call | solution.py:116
  8.2 65.7 %all_to_all.20.in_ref = f32[128,32,256]{2,1,0:T(8,128)S(1)} all-to-all(f32[128,32,256]{2,1,0:T(8,128)} %local_mix.1), channel_id=1, replica_groups=mesh['rows'=64,'sub'=2] {'rows','sub'}, dimensions={0} | all-to-all | bytes 8388608 | tf_op jit(solution)/shard_map/all_to_all | solution.py:351
  73.9 1.7 across_mix.1
  75.6 0.0 copy-start
  75.6 59.4 %all_to_all.21.values_ref = f32[128,2,32,128]{3,2,1,0:T(8,128)S(1)} all-to-all(f32[128,2,32,128]{3,2,1,0:T(8,128)S(1)} %across_mix.1), channel_id=1, replica_groups=mesh['rows'=64,'sub'=2] {'rows','sub'}, dimensions={0} | all-to-all | bytes 8388608 | tf_op jit(solution)/shard_map/all_to_all | solution.py:351
  135.0 0.0 copy-done
  135.0 4.3 %pick_rows.1 = (f32[128,32,256]{2,1,0:T(8,128)}, f32[128,3,4,128]{3,2,1,0:T(4,128)S(1)}) custom-call(s32[4,128]{1,0:T(4,128)S(1)} %bitcast.5, f32[128,2,32,128]{3,2,1,0:T(8,128)S(1)} %all_to_all.21.values_ref), custom_call_target="tpu_custom_call" | custom-call | tf_op jit(solution)/shard_map/pick_rows/pallas_call | solution.py:213
  139.3 20.9 %all_to_all.22.received_ref = f32[128,3,4,128]{3,2,1,0:T(4,128)S(1)} all-to-all(f32[128,3,4,128]{3,2,1,0:T(4,128)S(1)} %get-tuple-element.6), channel_id=1, replica_groups=mesh['rows'=64,'sub'=2] {'rows','sub'}, dimensions={0} | all-to-all | bytes 1572864 | tf_op jit(solution)/shard_map/all_to_all | solution.py:351
  160.2 0.9 sum_pieces.1
  161.1 5.4 %all-to-all-start.3 = ((f32[128,4,128]{2,1,0:T(4,128)}), f32[128,4,128]{2,1,0:T(4,128)S(1)}, u32[]{:S(2)}, u32[]{:S(2)}) async-start(f32[128,4,128]{2,1,0:T(4,128)} %sum_pieces.1), calls=%async_computation.3 | async-start | bytes 524288 | tf_op jit(solution)/shard_map/all_to_all | solution.py:351
  166.5 0.9 arrange_panel.1
  167.4 10.1 %all-to-all-done.3.refs_0_ = f32[128,4,128]{2,1,0:T(4,128)S(1)} async-done(((f32[128,4,128]{2,1,0:T(4,128)}), f32[128,4,128]{2,1,0:T(4,128)S(1)}, u32[]{:S(2)}, u32[]{:S(2)}) %all-to-all-start.3) | async-done | bytes 262176 | tf_op jit(solution)/shard_map/all_to_all | solution.py:351
  177.5 9.4 %upper_cholesky.1 = f32[256,256]{1,0:T(8,128)} custom-call(f32[128,4,128]{2,1,0:T(4,128)S(1)} %all-to-all-done.3.refs_0_), custom_call_target="tpu_custom_call" | custom-call | tf_op jit(solution)/shard_map/upper_cholesky/pallas_call | solution.py:339
Async XLA Ops:
  75.6 59.5 %copy-start = (s32[1,128,4]{1,2,0:T(4,128)S(1)}, s32[1,128,4]{1,2,0:T(4,128)}, u32[]{:S(2)}) copy-start(s32[1,128,4]{1,2,0:T(4,128)} %param.5) | copy-start | bytes 6148
  161.1 16.4 %all-to-all-start.3 = ((f32[128,4,128]{2,1,0:T(4,128)}), f32[128,4,128]{2,1,0:T(4,128)S(1)}, u32[]{:S(2)}, u32[]{:S(2)}) async-start(f32[128,4,128]{2,1,0:T(4,128)} %sum_pieces.1), calls=%async_computation.3 | async-start | bytes 524288 | tf_op jit(solution)/shard_map/all_to_all | solution.py:351

commit v3 on v2

--- a/solution.py
+++ b/solution.py
@@ -8,10 +8,12 @@
 from jax.sharding import PartitionSpec as P
 
 AXES = ("rows", "sub")
+ROUND = ("sub", "rows")
 TILE = 8
 RADIX = 8
-SUPER = 32
+SUPER = 64
 VMEM = 40 * 2**20
+SMALL = 16 * 2**20
 LARGE = 57 * 2**20
 
 
@@ -31,9 +33,9 @@
     return pl.BlockSpec(memory_space=space)
 
 
-def local_kernel(scale, matrix_ref, signs_ref, out_ref, came, first, second, third, flips, signs_held, sems):
+def local_kernel(scale, matrix_ref, signs_ref, out_ref, came, first, second, third, result, flips, signs_held, sems, out_sems):
     halves, length, _ = came.shape
-    share = out_ref.shape[1]
+    share = out_ref.shape[2]
     size = length // RADIX
     group = TILE * RADIX
     loads = [
@@ -98,35 +100,45 @@
 
         lax.fori_loop(0, group // TILE, outer, 0, unroll=2)
 
+    def send(q):
+        return pltpu.make_async_copy(result.at[:, q], out_ref.at[:, q], out_sems.at[q])
+
     def last(q, carry):
         for t in range(share // TILE):
             for h in range(halves):
                 at = pl.multiple_of(q * share, share) + t * TILE
                 parts = butterflies([third[h, pl.ds(c * size + at, TILE), :] for c in range(RADIX)])
                 for c in range(RADIX):
-                    out_ref[c * (size // share) + q, t * TILE:(t + 1) * TILE, h * 128:h * 128 + 128] = parts[c]
+                    result[c, q, t * TILE:(t + 1) * TILE, h * 128:h * 128 + 128] = parts[c]
+        send(q).start()
         return carry
 
     lax.fori_loop(0, size // share, last, 0)
+    for q in range(size // share):
+        send(q).wait()
 
 
 def local_mix(matrix_rows, signs, scale, owners):
     length, width = matrix_rows.shape
     halves = width // 128
-    return pl.pallas_call(
+    shape = (RADIX, owners // RADIX, length // owners, width)
+    mixed = pl.pallas_call(
         lambda *refs: local_kernel(scale, *refs),
-        out_shape=jax.ShapeDtypeStruct((owners, length // owners, width), jnp.float32),
+        out_shape=jax.ShapeDtypeStruct(shape, jnp.float32),
         in_specs=[whole(pltpu.HBM)] * 2,
-        out_specs=whole(),
+        out_specs=whole(pltpu.HBM),
         scratch_shapes=[pltpu.VMEM((halves, length, 128), jnp.float32)] * 4
         + [
+            pltpu.VMEM(shape, jnp.float32),
             pltpu.VMEM((length, 128), jnp.float32),
             pltpu.VMEM((length // 128, 128), jnp.int32),
             pltpu.SemaphoreType.DMA((RADIX * halves + 1,)),
+            pltpu.SemaphoreType.DMA((owners // RADIX,)),
         ],
         compiler_params=pltpu.CompilerParams(vmem_limit_bytes=LARGE),
         name="local_mix",
     )(matrix_rows, signs.reshape(length // 128, 128))
+    return mixed.reshape(owners, length // owners, width)
 
 
 def across_kernel(in_ref, out_ref, held):
@@ -164,65 +176,67 @@
     )(values)
 
 
-def pick_kernel(picks_ref, values_ref, mixed_ref, out_ref, taken, sems):
-    halves, rows = values_ref.shape[1], values_ref.shape[2]
+def turn(device, count):
+    return device % 2 * (count // 2) + device // 2
+
+
+def split(values):
+    high = values.astype(jnp.bfloat16)
+    rest = values - high.astype(jnp.float32)
+    middle = rest.astype(jnp.bfloat16)
+    low = (rest - middle.astype(jnp.float32)).astype(jnp.bfloat16)
+    return high, middle, low
+
+
+def square(block):
+    high, middle, low = split(block.T)
+    left = jnp.concatenate([high, low, middle, high, middle, high], axis=1)
+    high, middle, low = split(block)
+    right = jnp.concatenate([low, high, middle, middle, high, high], axis=0)
+    return left, right
+
+
+def pick_kernel(picks_ref, values_ref, out_ref, taken):
+    count, halves, rows, width = values_ref.shape
     tiles, _, slots, _ = taken.shape
-    each = out_ref.shape[2]
-    copies = [
-        pltpu.make_async_copy(
-            values_ref.at[:, half], mixed_ref.at[:, :, half * 128:half * 128 + 128], sems.at[half]
-        )
-        for half in range(halves)
-    ]
-    for copy in copies:
-        copy.start()
+    owners, _, each, _ = out_ref.shape
+    shift = rows.bit_length() - 1
+    flat = values_ref.reshape(count * halves * rows, width)
 
     def body(tile, carry):
         for slot in range(slots):
-            pick = picks_ref[slot % each, tile * (slots // each) + slot // each]
+            pair, place = slot // each, slot % each
+            pick = picks_ref[place, tile * 2 + pair]
             row = jnp.maximum(pick, 0)
+            at = (row >> shift) * (halves * rows) + (row & (rows - 1))
             for half in range(halves):
-                part = values_ref[row // rows, half, pl.ds(row % rows, 1), :]
-                taken[tile, half, slot:slot + 1, :] = jnp.where(pick >= 0, part, 0.0)
-        for half in range(halves):
-            for place in range(slots // each):
-                out_ref[tile * (slots // each) + place, half] = (
-                    taken[tile, half, place * each:(place + 1) * each, :]
-                )
+                part = jnp.where(pick >= 0, flat[pl.ds(at + half * rows, 1), :], 0.0)
+                taken[tile, half, slot:slot + 1, :] = part
+                out_ref[pair * (owners // 2) + tile, half, place:place + 1, :] = part
         return carry
 
-    lax.fori_loop(0, tiles, body, 0, unroll=2)
+    lax.fori_loop(0, tiles, body, 0, unroll=4)
     panel = jnp.concatenate([taken[:, half].reshape(-1, 128) for half in range(halves)], axis=1)
-    gram = lax.dot_general(
-        panel, panel, (((0,), (0,)), ((), ())),
-        precision=lax.Precision.HIGHEST, preferred_element_type=jnp.float32,
-    )
+    left, right = square(panel)
+    gram = jnp.dot(left, right, preferred_element_type=jnp.float32)
     each = gram.shape[0] // out_ref.shape[0]
     for owner in range(out_ref.shape[0]):
         for half in range(halves):
             out_ref[owner, halves, half * each:(half + 1) * each, :] = (
                 gram[owner * each:(owner + 1) * each, half * 128:half * 128 + 128]
             )
-    for copy in copies:
-        copy.wait()
 
 
 def pick_rows(values, picks):
-    count, halves, rows, _ = values.shape
+    halves = values.shape[1]
     slots, owners = picks.shape
     return pl.pallas_call(
         pick_kernel,
-        out_shape=(
-            jax.ShapeDtypeStruct((count, rows, halves * 128), jnp.float32),
-            jax.ShapeDtypeStruct((owners, halves + 1, slots, 128), jnp.float32),
-        ),
+        out_shape=jax.ShapeDtypeStruct((owners, halves + 1, slots, 128), jnp.float32),
         in_specs=[whole(pltpu.SMEM), whole()],
-        out_specs=(whole(pltpu.HBM), whole()),
-        scratch_shapes=[
-            pltpu.VMEM((slots * owners // TILE, halves, TILE, 128), jnp.float32),
-            pltpu.SemaphoreType.DMA((halves,)),
-        ],
-        compiler_params=pltpu.CompilerParams(vmem_limit_bytes=VMEM),
+        out_specs=whole(),
+        scratch_shapes=[pltpu.VMEM((slots * owners // TILE, halves, TILE, 128), jnp.float32)],
+        compiler_params=pltpu.CompilerParams(vmem_limit_bytes=SMALL),
         name="pick_rows",
     )(picks, values)
 
@@ -245,30 +259,25 @@
     )(received)
 
 
-def panel_kernel(received_ref, panel_ref):
-    sources, last, slots, _ = received_ref.shape
-    for source in range(sources):
-        for half in range(last - 1):
-            panel_ref[source * slots:(source + 1) * slots, half * 128:half * 128 + 128] = (
-                received_ref[source, half]
-            )
-
-
-def arrange_panel(received):
-    sources, last, slots, width = received.shape
-    return pl.pallas_call(
-        panel_kernel,
-        out_shape=jax.ShapeDtypeStruct((sources * slots, (last - 1) * width), jnp.float32),
-        in_specs=[whole()],
-        out_specs=whole(),
-        compiler_params=pltpu.CompilerParams(vmem_limit_bytes=VMEM),
-        name="arrange_panel",
-    )(received)
-
-
-def cholesky_kernel(expected, pieces_ref, out_ref, held):
+def finish_kernel(expected, pieces_ref, received_ref, values_ref, mixed_ref, panel_ref, out_ref, held, panel, sems):
     size = held.shape[0]
     halves = size // 128
+    copies = [
+        pltpu.make_async_copy(
+            values_ref.at[:, half], mixed_ref.at[:, :, half * 128:half * 128 + 128], sems.at[half]
+        )
+        for half in range(halves)
+    ]
+    copies.append(pltpu.make_async_copy(panel, panel_ref, sems.at[halves]))
+    for copy in copies[:halves]:
+        copy.start()
+    sources, _, slots, _ = received_ref.shape
+    for source in range(sources):
+        for half in range(halves):
+            panel[source * slots:(source + 1) * slots, half * 128:half * 128 + 128] = (
+                received_ref[turn(source, sources), half]
+            )
+    copies[halves].start()
     each = pieces_ref.shape[1] // halves
     for owner in range(pieces_ref.shape[0]):
         for half in range(halves):
@@ -327,28 +336,38 @@
             block = jnp.concatenate(
                 [jnp.concatenate(rows[t], axis=1) for t in range(tiles)], axis=0
             )
-            turned = block.T[after:]
-            held[after:, :] -= jnp.dot(
-                turned, block, precision=lax.Precision.HIGHEST, preferred_element_type=jnp.float32
-            )
-
-
-def upper_cholesky(pieces, expected):
+            left, right = square(block)
+            held[after:, :] -= jnp.dot(left[after:], right, preferred_element_type=jnp.float32)
+    for copy in copies:
+        copy.wait()
+
+
+def finish(pieces, received, values, expected):
     owners, rows, width = pieces.shape
-    size = math.isqrt(owners * rows * width)
+    count, halves, share, _ = values.shape
+    size = halves * width
+    panel = jax.ShapeDtypeStruct((received.shape[0] * received.shape[2], size), jnp.float32)
     return pl.pallas_call(
-        lambda *refs: cholesky_kernel(expected, *refs),
-        out_shape=jax.ShapeDtypeStruct((size, size), jnp.float32),
-        in_specs=[whole()],
-        out_specs=whole(),
-        scratch_shapes=[pltpu.VMEM((size, size), jnp.float32)],
-        compiler_params=pltpu.CompilerParams(vmem_limit_bytes=VMEM),
-        name="upper_cholesky",
-    )(pieces)
+        lambda *refs: finish_kernel(expected, *refs),
+        out_shape=(
+            jax.ShapeDtypeStruct((count, share, size), jnp.float32),
+            panel,
+            jax.ShapeDtypeStruct((size, size), jnp.float32),
+        ),
+        in_specs=[whole()] * 3,
+        out_specs=(whole(pltpu.HBM), whole(pltpu.HBM), whole()),
+        scratch_shapes=[
+            pltpu.VMEM((size, size), jnp.float32),
+            pltpu.VMEM(panel.shape, jnp.float32),
+            pltpu.SemaphoreType.DMA((halves + 1,)),
+        ],
+        compiler_params=pltpu.CompilerParams(vmem_limit_bytes=SMALL),
+        name="finish",
+    )(pieces, received, values)
 
 
 def exchange(block):
-    return lax.all_to_all(block, AXES, split_axis=0, concat_axis=0, tiled=True)
+    return lax.all_to_all(block, ROUND, split_axis=0, concat_axis=0, tiled=True)
 
 
 def on_device(matrix_rows, signs, picks):
@@ -359,11 +378,9 @@
     expected = owners * owners * slots / 2.0
 
     values = exchange(across_mix(exchange(local_mix(matrix_rows, signs, scale, owners))))
-    mixed, taken = pick_rows(values, picks[0].T)
-    received = exchange(taken)
+    received = exchange(pick_rows(values, picks[0].T))
     pieces = exchange(sum_pieces(received))
-    factor = upper_cholesky(pieces, expected)
-    panel = arrange_panel(received)
+    mixed, panel, factor = finish(pieces, received, values, expected)
     return (mixed.reshape(length, width), panel, factor)
 
 

time: 187 us -> 180 us (0.963)
  blocking collectives: 146 us -> 158 us
  waiting for transfers between devices: 10.1 us -> 0 us
  starting transfers between devices: 5.36 us -> 0 us
  Pallas kernels: 24.7 us -> 21.5 us
    all_to_all x3 -> x4, blocking collectives: 146 us -> 158 us  [exchange(): return lax.all_to_all(block, ROUND, split_axis=0, concat_axis=0, tiled=True)]
    all_to_all x1 -> x0, waiting for transfers between devices: 10.1 us -> none  [exchange(): return lax.all_to_all(block, AXES, split_axis=0, concat_axis=0, tiled=True)]
    all_to_all x1 -> x0, starting transfers between devices: 5.36 us -> none  [exchange(): return lax.all_to_all(block, AXES, split_axis=0, concat_axis=0, tiled=True)]
    pallas_call x3 -> x2, Pallas kernels: 14.6 us -> 12.5 us  [the longest x1 9.32 us: finish(): pl.pallas_call(lambda *refs: finish_kernel(expected, *refs), out_shape=(j...]
  transfers between devices with their start and end apart: 1 -> 0, of which waited for: 1 -> 0; matrix products, arithmetic and copies ran while one was open for 0% -> 0% of each run, Pallas kernels for 0% -> 0%
where the time goes in v3:
time: 180 us
  blocking collectives  158 us (88%)
  Pallas kernels  21.5 us (12%)
    all_to_all x4, blocking collectives, exchange(): return lax.all_to_all(block, ROUND, split_axis=0, concat_axis=0, tiled=True)  158 us
    pallas_call x1, Pallas kernels, finish(): pl.pallas_call(lambda *refs: finish_kernel(expected, *refs), out_shape=(j...  9.32 us
    pallas_call x1, Pallas kernels, local_mix(): pl.pallas_call(lambda *refs: local_kernel(scale, *refs), out_shape=jax.Sh...  7.11 us

profile of v3, /device:TPU:1, one launch (start us, length us, event | category | flops | bytes accessed | tf_op | source)
XLA Modules:
  0.0 179.8 jit_solution(18369623167060933476)
XLA Ops:
  0.6 7.1 %local_mix.1 = f32[8,16,32,256]{3,2,1,0:T(8,128)} custom-call(f32[4096,256]{1,0:T(8,128)} %refs_0_.1, s32[32,128]{1,0:T(8,128)} %bitcast.8), custom_call_target="tpu_custom_call" | custom-call | tf_op jit(solution)/shard_map/local_mix/pallas_call | solution.py:125
  7.8 64.5 %all_to_all.20.in_ref = f32[128,32,256]{2,1,0:T(8,128)S(1)} all-to-all(f32[128,32,256]{2,1,0:T(8,128)} %bitcast.7), channel_id=1, replica_groups=mesh['rows'=64,'sub'=2] {'sub','rows'}, dimensions={0} | all-to-all | bytes 8388608 | tf_op jit(solution)/shard_map/all_to_all | solution.py:370
  72.2 1.7 across_mix.1
  73.9 0.0 copy-start
  73.9 57.3 %all_to_all.21.values_ref.refs_2_ = f32[128,2,32,128]{3,2,1,0:T(8,128)S(1)} all-to-all(f32[128,2,32,128]{3,2,1,0:T(8,128)S(1)} %across_mix.1), channel_id=1, replica_groups=mesh['rows'=64,'sub'=2] {'sub','rows'}, dimensions={0} | all-to-all | bytes 8388608 | tf_op jit(solution)/shard_map/all_to_all | solution.py:370
  131.2 0.0 copy-done
  131.2 3.2 %pick_rows.1 = f32[128,3,4,128]{3,2,1,0:T(4,128)S(1)} custom-call(s32[4,128]{1,0:T(4,128)S(1)} %bitcast.6, f32[128,2,32,128]{3,2,1,0:T(8,128)S(1)} %all_to_all.21.values_ref.refs_2_), custom_call_target="tpu_custom_call" | custom-call | tf_op jit(solution)/shard_map/pick_rows/pallas_call | solution.py:233
  134.4 20.7 %all_to_all.22.received_ref.refs_1_ = f32[128,3,4,128]{3,2,1,0:T(4,128)S(1)} all-to-all(f32[128,3,4,128]{3,2,1,0:T(4,128)S(1)} %pick_rows.1), channel_id=1, replica_groups=mesh['rows'=64,'sub'=2] {'sub','rows'}, dimensions={0} | all-to-all | bytes 1572864 | tf_op jit(solution)/shard_map/all_to_all | solution.py:370
  155.1 0.2 sum_pieces.1
  155.3 15.2 %all_to_all.23.refs_0_ = f32[128,4,128]{2,1,0:T(4,128)S(1)} all-to-all(f32[128,4,128]{2,1,0:T(4,128)S(1)} %sum_pieces.1), channel_id=1, replica_groups=mesh['rows'=64,'sub'=2] {'sub','rows'}, dimensions={0} | all-to-all | bytes 524288 | tf_op jit(solution)/shard_map/all_to_all | solution.py:370
  170.5 9.3 %finish.1 = (f32[128,32,256]{2,1,0:T(8,128)}, f32[512,256]{1,0:T(8,128)}, f32[256,256]{1,0:T(8,128)}) custom-call(f32[128,4,128]{2,1,0:T(4,128)S(1)} %all_to_all.23.refs_0_, f32[128,3,4,128]{3,2,1,0:T(4,128)S(1)} %all_to_all.22.received_ref.refs_1_, f32[128,2,32,128]{3,2,1,0:T(8,128)S(1)} %all_to_all.21.values_ref.refs_2_), custom_call_target="tpu_custom_call" | custom-call | tf_op jit(solution)/shard_map/finish/pallas_call | solution.py:350
Async XLA Ops:
  73.9 57.3 %copy-start = (s32[1,128,4]{1,2,0:T(4,128)S(1)}, s32[1,128,4]{1,2,0:T(4,128)}, u32[]{:S(2)}) copy-start(s32[1,128,4]{1,2,0:T(4,128)} %param.5) | copy-start | bytes 6148

commit v4 on v3

--- a/solution.py
+++ b/solution.py
@@ -5,12 +5,14 @@
 from jax import lax
 from jax.experimental import pallas as pl
 from jax.experimental.pallas import tpu as pltpu
-from jax.sharding import PartitionSpec as P
-
-AXES = ("rows", "sub")
-ROUND = ("sub", "rows")
+from jax.sharding import Mesh, PartitionSpec as P
+
+AXES = ("y_low", "x", "z", "core", "y_high")
+SIZES = (2, 4, 4, 2, 2)
+ROUND = ("z", "y_high", "y_low", "x", "core")
 TILE = 8
 RADIX = 8
+AT_ONCE = 16
 SUPER = 64
 VMEM = 40 * 2**20
 SMALL = 16 * 2**20
@@ -68,7 +70,7 @@
         )
         return carry
 
-    lax.fori_loop(0, length // 128, flip, 0, unroll=4)
+    lax.fori_loop(0, length // 128, flip, 0, unroll=16)
 
     for c in range(RADIX):
         for load in loads[c]:
@@ -88,7 +90,7 @@
                     second[h, pl.ds(base + TILE * t, TILE), :] = parts[t]
             return carry
 
-        lax.fori_loop(0, size // group, inner, 0, unroll=2)
+        lax.fori_loop(0, size // group, inner, 0, unroll=8)
 
         def outer(t, carry):
             base = pl.multiple_of(c * size + t * TILE, TILE)
@@ -98,7 +100,7 @@
                     third[h, pl.ds(base + group * g, TILE), :] = parts[g]
             return carry
 
-        lax.fori_loop(0, group // TILE, outer, 0, unroll=2)
+        lax.fori_loop(0, group // TILE, outer, 0, unroll=8)
 
     def send(q):
         return pltpu.make_async_copy(result.at[:, q], out_ref.at[:, q], out_sems.at[q])
@@ -113,7 +115,7 @@
         send(q).start()
         return carry
 
-    lax.fori_loop(0, size // share, last, 0)
+    lax.fori_loop(0, size // share, last, 0, unroll=2)
     for q in range(size // share):
         send(q).wait()
 
@@ -176,8 +178,16 @@
     )(values)
 
 
-def turn(device, count):
-    return device % 2 * (count // 2) + device // 2
+def turn(device):
+    weights, weight = {}, 1
+    for axis in reversed(ROUND):
+        weights[axis] = weight
+        weight *= SIZES[AXES.index(axis)]
+    place = 0
+    for axis, size in zip(reversed(AXES), reversed(SIZES)):
+        place = place + (device & (size - 1)) * weights[axis]
+        device = device >> (size.bit_length() - 1)
+    return place
 
 
 def split(values):
@@ -188,10 +198,10 @@
     return high, middle, low
 
 
-def square(block):
-    high, middle, low = split(block.T)
-    left = jnp.concatenate([high, low, middle, high, middle, high], axis=1)
-    high, middle, low = split(block)
+def factors(parts, others, axis):
+    high, middle, low = parts
+    left = jnp.concatenate([high, low, middle, high, middle, high], axis=axis)
+    high, middle, low = others
     right = jnp.concatenate([low, high, middle, middle, high, high], axis=0)
     return left, right
 
@@ -203,21 +213,24 @@
     shift = rows.bit_length() - 1
     flat = values_ref.reshape(count * halves * rows, width)
 
-    def body(tile, carry):
-        for slot in range(slots):
-            pair, place = slot // each, slot % each
-            pick = picks_ref[place, tile * 2 + pair]
-            row = jnp.maximum(pick, 0)
-            at = (row >> shift) * (halves * rows) + (row & (rows - 1))
-            for half in range(halves):
-                part = jnp.where(pick >= 0, flat[pl.ds(at + half * rows, 1), :], 0.0)
-                taken[tile, half, slot:slot + 1, :] = part
-                out_ref[pair * (owners // 2) + tile, half, place:place + 1, :] = part
+    def body(step, carry):
+        first = turn(step * (2 * AT_ONCE))
+        for number in range(AT_ONCE):
+            tile = step * AT_ONCE + number
+            for slot in range(slots):
+                pair, place = number * 2 + slot // each, slot % each
+                pick = picks_ref[place, step * (2 * AT_ONCE) + pair]
+                row = jnp.maximum(pick, 0)
+                at = (row >> shift) * (halves * rows) + (row & (rows - 1))
+                for half in range(halves):
+                    part = jnp.where(pick >= 0, flat[pl.ds(at + half * rows, 1), :], 0.0)
+                    taken[tile, half, slot:slot + 1, :] = part
+                    out_ref[first + turn(pair), half, place:place + 1, :] = part
         return carry
 
-    lax.fori_loop(0, tiles, body, 0, unroll=4)
+    lax.fori_loop(0, tiles // AT_ONCE, body, 0)
     panel = jnp.concatenate([taken[:, half].reshape(-1, 128) for half in range(halves)], axis=1)
-    left, right = square(panel)
+    left, right = factors(split(panel.T), split(panel), 1)
     gram = jnp.dot(left, right, preferred_element_type=jnp.float32)
     each = gram.shape[0] // out_ref.shape[0]
     for owner in range(out_ref.shape[0]):
@@ -239,24 +252,6 @@
         compiler_params=pltpu.CompilerParams(vmem_limit_bytes=SMALL),
         name="pick_rows",
     )(picks, values)
-
-
-def sum_kernel(received_ref, out_ref):
-    sources, last = received_ref.shape[0], received_ref.shape[1] - 1
-    total = jnp.sum(received_ref[:, last], axis=0)
-    out_ref[...] = jnp.broadcast_to(total[None], out_ref.shape)
-
-
-def sum_pieces(received):
-    sources, _, rows, width = received.shape
-    return pl.pallas_call(
-        sum_kernel,
-        out_shape=jax.ShapeDtypeStruct((sources, rows, width), jnp.float32),
-        in_specs=[whole()],
-        out_specs=whole(),
-        compiler_params=pltpu.CompilerParams(vmem_limit_bytes=VMEM),
-        name="sum_pieces",
-    )(received)
 
 
 def finish_kernel(expected, pieces_ref, received_ref, values_ref, mixed_ref, panel_ref, out_ref, held, panel, sems):
@@ -275,7 +270,7 @@
     for source in range(sources):
         for half in range(halves):
             panel[source * slots:(source + 1) * slots, half * 128:half * 128 + 128] = (
-                received_ref[turn(source, sources), half]
+                received_ref[turn(source), half]
             )
     copies[halves].start()
     each = pieces_ref.shape[1] // halves
@@ -336,8 +331,8 @@
             block = jnp.concatenate(
                 [jnp.concatenate(rows[t], axis=1) for t in range(tiles)], axis=0
             )
-            left, right = square(block)
-            held[after:, :] -= jnp.dot(left[after:], right, preferred_element_type=jnp.float32)
+            left, right = factors(split(block), split(block), 0)
+            held[after:, :] -= jnp.dot(left.T[after:], right, preferred_element_type=jnp.float32)
     for copy in copies:
         copy.wait()
 
@@ -372,14 +367,15 @@
 
 def on_device(matrix_rows, signs, picks):
     length, width = matrix_rows.shape
-    owners = lax.axis_size("rows") * lax.axis_size("sub")
+    owners = math.prod(SIZES)
     slots = picks.shape[2]
     scale = 1.0 / math.sqrt(length * owners)
     expected = owners * owners * slots / 2.0
 
     values = exchange(across_mix(exchange(local_mix(matrix_rows, signs, scale, owners))))
     received = exchange(pick_rows(values, picks[0].T))
-    pieces = exchange(sum_pieces(received))
+    piece = jnp.sum(received[:, -1], axis=0)
+    pieces = exchange(jnp.broadcast_to(piece, (owners,) + piece.shape))
     mixed, panel, factor = finish(pieces, received, values, expected)
     return (mixed.reshape(length, width), panel, factor)
 
@@ -388,7 +384,7 @@
     placed = (P(AXES, None), P(AXES), P(AXES, None, None))
     return jax.shard_map(
         on_device,
-        mesh=mesh,
+        mesh=Mesh(mesh.devices.reshape(SIZES), AXES),
         in_specs=placed,
         out_specs=(P(AXES, None), P(AXES, None), P()),
         check_vma=False,

time: 180 us -> 178 us (0.989)
  no operation moved by 1% of the time
where the time goes in v4:
time: 178 us
  blocking collectives  157 us (88%)
  Pallas kernels  19.9 us (11%)
    all_to_all x4, blocking collectives, exchange(): return lax.all_to_all(block, ROUND, split_axis=0, concat_axis=0, tiled=True)  157 us
    pallas_call x1, Pallas kernels, finish(): pl.pallas_call(lambda *refs: finish_kernel(expected, *refs), out_shape=(j...  9.07 us
    pallas_call x1, Pallas kernels, local_mix(): pl.pallas_call(lambda *refs: local_kernel(scale, *refs), out_shape=jax.Sh...  5.98 us

profile of v4, /device:TPU:1, one launch (start us, length us, event | category | flops | bytes accessed | tf_op | source)
XLA Modules:
  0.0 177.9 jit_solution(3691968259340630606)
XLA Ops:
  0.6 6.0 %local_mix.1 = f32[8,16,32,256]{3,2,1,0:T(8,128)} custom-call(f32[4096,256]{1,0:T(8,128)} %refs_0_.1, s32[32,128]{1,0:T(8,128)} %bitcast.8), custom_call_target="tpu_custom_call" | custom-call | tf_op jit(solution)/shard_map/local_mix/pallas_call | solution.py:127
  6.6 64.5 %all_to_all.20.in_ref = f32[128,32,256]{2,1,0:T(8,128)S(1)} all-to-all(f32[128,32,256]{2,1,0:T(8,128)} %bitcast.7), channel_id=1, replica_groups=mesh['y_low'=2,'x'=4,'z'=4,'core'=2,'y_high'=2] {'z','y_high','y_low','x..., dimensions={0} | all-to-all | bytes 8388608 | tf_op jit(solution)/shard_map/all_to_all | solution.py:365
  71.1 1.7 across_mix.1
  72.8 0.0 copy-start
  72.8 56.9 %all_to_all.21.values_ref.refs_2_ = f32[128,2,32,128]{3,2,1,0:T(8,128)S(1)} all-to-all(f32[128,2,32,128]{3,2,1,0:T(8,128)S(1)} %across_mix.1), channel_id=1, replica_groups=mesh['y_low'=2,'x'=4,'z'=4,'core'=2,'y_high'=2] {'z','y_high','y_low','x..., dimensions={0} | all-to-all | bytes 8388608 | tf_op jit(solution)/shard_map/all_to_all | solution.py:365
  129.7 0.0 copy-done
  129.7 3.1 %pick_rows.1 = f32[128,3,4,128]{3,2,1,0:T(4,128)S(1)} custom-call(s32[4,128]{1,0:T(4,128)S(1)} %bitcast.6, f32[128,2,32,128]{3,2,1,0:T(8,128)S(1)} %all_to_all.21.values_ref.refs_2_), custom_call_target="tpu_custom_call" | custom-call | tf_op jit(solution)/shard_map/pick_rows/pallas_call | solution.py:246
  132.9 20.4 %all_to_all.22.refs_1_ = f32[128,3,4,128]{3,2,1,0:T(4,128)S(1)} all-to-all(f32[128,3,4,128]{3,2,1,0:T(4,128)S(1)} %pick_rows.1), channel_id=1, replica_groups=mesh['y_low'=2,'x'=4,'z'=4,'core'=2,'y_high'=2] {'z','y_high','y_low','x..., dimensions={0} | all-to-all | bytes 1572864 | tf_op jit(solution)/shard_map/all_to_all | solution.py:365
  153.2 0.1 slice_reduce_fusion
  153.4 15.4 %all_to_all.23.refs_0_ = f32[128,4,128]{2,1,0:T(4,128)S(1)} all-to-all(f32[128,4,128]{2,1,0:T(4,128)S(1)} %broadcast_in_dim.3), channel_id=1, replica_groups=mesh['y_low'=2,'x'=4,'z'=4,'core'=2,'y_high'=2] {'z','y_high','y_low','x..., dimensions={0} | all-to-all | bytes 524288 | tf_op jit(solution)/shard_map/all_to_all | solution.py:365
  168.9 9.1 %finish.1 = (f32[128,32,256]{2,1,0:T(8,128)}, f32[512,256]{1,0:T(8,128)}, f32[256,256]{1,0:T(8,128)}) custom-call(f32[128,4,128]{2,1,0:T(4,128)S(1)} %all_to_all.23.refs_0_, f32[128,3,4,128]{3,2,1,0:T(4,128)S(1)} %all_to_all.22.refs_1_, f32[128,2,32,128]{3,2,1,0:T(8,128)S(1)} %all_to_all.21.values_ref.refs_2_), custom_call_target="tpu_custom_call" | custom-call | tf_op jit(solution)/shard_map/finish/pallas_call | solution.py:345
  (1 shorter events, 0.0 us)
Async XLA Ops:
  72.8 56.9 %copy-start = (s32[1,128,4]{1,2,0:T(4,128)S(1)}, s32[1,128,4]{1,2,0:T(4,128)}, u32[]{:S(2)}) copy-start(s32[1,128,4]{1,2,0:T(4,128)} %param.5) | copy-start | bytes 6148

commit v5 on v4

--- a/solution.py
+++ b/solution.py
@@ -9,10 +9,11 @@
 
 AXES = ("y_low", "x", "z", "core", "y_high")
 SIZES = (2, 4, 4, 2, 2)
-ROUND = ("z", "y_high", "y_low", "x", "core")
+ROUND = ("z", "core", "x", "y_high", "y_low")
 TILE = 8
 RADIX = 8
 AT_ONCE = 16
+MOVES = 4
 SUPER = 64
 VMEM = 40 * 2**20
 SMALL = 16 * 2**20
@@ -257,6 +258,7 @@
 def finish_kernel(expected, pieces_ref, received_ref, values_ref, mixed_ref, panel_ref, out_ref, held, panel, sems):
     size = held.shape[0]
     halves = size // 128
+    each = pieces_ref.shape[1] // halves
     copies = [
         pltpu.make_async_copy(
             values_ref.at[:, half], mixed_ref.at[:, :, half * 128:half * 128 + 128], sems.at[half]
@@ -267,18 +269,25 @@
     for copy in copies[:halves]:
         copy.start()
     sources, _, slots, _ = received_ref.shape
-    for source in range(sources):
+
+    def move_rows(owner):
+        for half in range(halves):
+            held[owner * each:(owner + 1) * each, half * 128:half * 128 + 128] = (
+                pieces_ref[owner, half * each:(half + 1) * each, :] * (1.0 / expected)
+            )
+
+    def move_panel(source):
         for half in range(halves):
             panel[source * slots:(source + 1) * slots, half * 128:half * 128 + 128] = (
                 received_ref[turn(source), half]
             )
-    copies[halves].start()
-    each = pieces_ref.shape[1] // halves
-    for owner in range(pieces_ref.shape[0]):
-        for half in range(halves):
-            held[owner * each:(owner + 1) * each, half * 128:half * 128 + 128] = (
-                pieces_ref[owner, half * each:(half + 1) * each, :] * (1.0 / expected)
-            )
+
+    first_owners = SUPER // each
+    for owner in range(first_owners):
+        move_rows(owner)
+    moves = [(move_rows, owner) for owner in range(first_owners, pieces_ref.shape[0])]
+    moves += [(move_panel, source) for source in range(sources)]
+
     place = lax.broadcasted_iota(jnp.int32, (TILE, 128), 0)
     lane = lax.broadcasted_iota(jnp.int32, (TILE, 128), 1)
 
@@ -303,6 +312,9 @@
             }
             finished = list(rows[t])
             for k in range(TILE):
+                for move, number in moves[:MOVES]:
+                    move(number)
+                moves = moves[MOVES:]
                 pivot = spread_row(edges[t][k], k)
                 inverse = 1.0 / pivot
                 root = lax.rsqrt(pivot)
@@ -326,6 +338,11 @@
             ]
             for h in range(halves):
                 out_ref[first:first + TILE, h * 128:h * 128 + 128] = rows[t][h]
+        if base == 0:
+            for move, number in moves:
+                move(number)
+            moves = []
+            copies[halves].start()
         after = base + SUPER
         if after < size:
             block = jnp.concatenate(

time: 178 us -> 177 us (level)
  no operation moved by 1% of the time
where the time goes in v5:
time: 177 us
  blocking collectives  156 us (88%)
  Pallas kernels  19.9 us (11%)
    all_to_all x4, blocking collectives, exchange(): return lax.all_to_all(block, ROUND, split_axis=0, concat_axis=0, tiled=True)  156 us
    pallas_call x1, Pallas kernels, finish(): pl.pallas_call(lambda *refs: finish_kernel(expected, *refs), out_shape=(j...  9.07 us
    pallas_call x1, Pallas kernels, local_mix(): pl.pallas_call(lambda *refs: local_kernel(scale, *refs), out_shape=jax.Sh...  5.98 us

profile of v5, /device:TPU:1, one launch (start us, length us, event | category | flops | bytes accessed | tf_op | source)
XLA Modules:
  0.0 177.1 jit_solution(12634751736871123447)
XLA Ops:
  0.6 6.0 %local_mix.1 = f32[8,16,32,256]{3,2,1,0:T(8,128)} custom-call(f32[4096,256]{1,0:T(8,128)} %refs_0_.1, s32[32,128]{1,0:T(8,128)} %bitcast.8), custom_call_target="tpu_custom_call" | custom-call | tf_op jit(solution)/shard_map/local_mix/pallas_call | solution.py:128
  6.6 64.2 %all_to_all.20.in_ref = f32[128,32,256]{2,1,0:T(8,128)S(1)} all-to-all(f32[128,32,256]{2,1,0:T(8,128)} %bitcast.7), channel_id=1, replica_groups=mesh['y_low'=2,'x'=4,'z'=4,'core'=2,'y_high'=2] {'z','core','x','y_high'..., dimensions={0} | all-to-all | bytes 8388608 | tf_op jit(solution)/shard_map/all_to_all | solution.py:382
  70.8 1.7 across_mix.1
  72.5 0.0 copy-start
  72.5 56.7 %all_to_all.21.values_ref.refs_2_ = f32[128,2,32,128]{3,2,1,0:T(8,128)S(1)} all-to-all(f32[128,2,32,128]{3,2,1,0:T(8,128)S(1)} %across_mix.1), channel_id=1, replica_groups=mesh['y_low'=2,'x'=4,'z'=4,'core'=2,'y_high'=2] {'z','core','x','y_high'..., dimensions={0} | all-to-all | bytes 8388608 | tf_op jit(solution)/shard_map/all_to_all | solution.py:382
  129.2 0.0 copy-done
  129.2 3.1 %pick_rows.1 = f32[128,3,4,128]{3,2,1,0:T(4,128)S(1)} custom-call(s32[4,128]{1,0:T(4,128)S(1)} %bitcast.6, f32[128,2,32,128]{3,2,1,0:T(8,128)S(1)} %all_to_all.21.values_ref.refs_2_), custom_call_target="tpu_custom_call" | custom-call | tf_op jit(solution)/shard_map/pick_rows/pallas_call | solution.py:247
  132.4 20.0 %all_to_all.22.refs_1_ = f32[128,3,4,128]{3,2,1,0:T(4,128)S(1)} all-to-all(f32[128,3,4,128]{3,2,1,0:T(4,128)S(1)} %pick_rows.1), channel_id=1, replica_groups=mesh['y_low'=2,'x'=4,'z'=4,'core'=2,'y_high'=2] {'z','core','x','y_high'..., dimensions={0} | all-to-all | bytes 1572864 | tf_op jit(solution)/shard_map/all_to_all | solution.py:382
  152.4 0.1 slice_reduce_fusion
  152.5 15.5 %all_to_all.23.refs_0_ = f32[128,4,128]{2,1,0:T(4,128)S(1)} all-to-all(f32[128,4,128]{2,1,0:T(4,128)S(1)} %broadcast_in_dim.3), channel_id=1, replica_groups=mesh['y_low'=2,'x'=4,'z'=4,'core'=2,'y_high'=2] {'z','core','x','y_high'..., dimensions={0} | all-to-all | bytes 524288 | tf_op jit(solution)/shard_map/all_to_all | solution.py:382
  168.0 9.1 %finish.1 = (f32[128,32,256]{2,1,0:T(8,128)}, f32[512,256]{1,0:T(8,128)}, f32[256,256]{1,0:T(8,128)}) custom-call(f32[128,4,128]{2,1,0:T(4,128)S(1)} %all_to_all.23.refs_0_, f32[128,3,4,128]{3,2,1,0:T(4,128)S(1)} %all_to_all.22.refs_1_, f32[128,2,32,128]{3,2,1,0:T(8,128)S(1)} %all_to_all.21.values_ref.refs_2_), custom_call_target="tpu_custom_call" | custom-call | tf_op jit(solution)/shard_map/finish/pallas_call | solution.py:362
  (1 shorter events, 0.0 us)
Async XLA Ops:
  72.5 56.7 %copy-start = (s32[1,128,4]{1,2,0:T(4,128)S(1)}, s32[1,128,4]{1,2,0:T(4,128)}, u32[]{:S(2)}) copy-start(s32[1,128,4]{1,2,0:T(4,128)} %param.5) | copy-start | bytes 6148

commit v6 on v5

--- a/solution.py
+++ b/solution.py
@@ -17,7 +17,7 @@
 SUPER = 64
 VMEM = 40 * 2**20
 SMALL = 16 * 2**20
-LARGE = 57 * 2**20
+LARGE = 48 * 2**20
 
 
 def butterflies(parts):
@@ -36,7 +36,7 @@
     return pl.BlockSpec(memory_space=space)
 
 
-def local_kernel(scale, matrix_ref, signs_ref, out_ref, came, first, second, third, result, flips, signs_held, sems, out_sems):
+def local_kernel(scale, matrix_ref, signs_ref, out_ref, came, first, second, third, flips, signs_held, sems):
     halves, length, _ = came.shape
     share = out_ref.shape[2]
     size = length // RADIX
@@ -103,22 +103,16 @@
 
         lax.fori_loop(0, group // TILE, outer, 0, unroll=8)
 
-    def send(q):
-        return pltpu.make_async_copy(result.at[:, q], out_ref.at[:, q], out_sems.at[q])
-
     def last(q, carry):
         for t in range(share // TILE):
             for h in range(halves):
                 at = pl.multiple_of(q * share, share) + t * TILE
                 parts = butterflies([third[h, pl.ds(c * size + at, TILE), :] for c in range(RADIX)])
                 for c in range(RADIX):
-                    result[c, q, t * TILE:(t + 1) * TILE, h * 128:h * 128 + 128] = parts[c]
-        send(q).start()
+                    out_ref[c, q, t * TILE:(t + 1) * TILE, h * 128:h * 128 + 128] = parts[c]
         return carry
 
     lax.fori_loop(0, size // share, last, 0, unroll=2)
-    for q in range(size // share):
-        send(q).wait()
 
 
 def local_mix(matrix_rows, signs, scale, owners):
@@ -129,14 +123,12 @@
         lambda *refs: local_kernel(scale, *refs),
         out_shape=jax.ShapeDtypeStruct(shape, jnp.float32),
         in_specs=[whole(pltpu.HBM)] * 2,
-        out_specs=whole(pltpu.HBM),
+        out_specs=whole(),
         scratch_shapes=[pltpu.VMEM((halves, length, 128), jnp.float32)] * 4
         + [
-            pltpu.VMEM(shape, jnp.float32),
             pltpu.VMEM((length, 128), jnp.float32),
             pltpu.VMEM((length // 128, 128), jnp.int32),
             pltpu.SemaphoreType.DMA((RADIX * halves + 1,)),
-            pltpu.SemaphoreType.DMA((owners // RADIX,)),
         ],
         compiler_params=pltpu.CompilerParams(vmem_limit_bytes=LARGE),
         name="local_mix",

time: 177 us -> 176 us (level)
  Pallas kernels: 19.9 us -> 17.9 us
    pallas_call x1, Pallas kernels: 5.98 us -> 4.04 us  [local_mix(): pl.pallas_call(lambda *refs: local_kernel(scale, *refs), out_shape=jax.Sh...]
where the time goes in v6:
time: 176 us
  blocking collectives  156 us (89%)
  Pallas kernels  17.9 us (10%)
    all_to_all x4, blocking collectives, exchange(): return lax.all_to_all(block, ROUND, split_axis=0, concat_axis=0, tiled=True)  156 us
    pallas_call x1, Pallas kernels, finish(): pl.pallas_call(lambda *refs: finish_kernel(expected, *refs), out_shape=(j...  9.07 us
    pallas_call x1, Pallas kernels, local_mix(): pl.pallas_call(lambda *refs: local_kernel(scale, *refs), out_shape=jax.Sh...  4.04 us

profile of v6, /device:TPU:1, one launch (start us, length us, event | category | flops | bytes accessed | tf_op | source)
XLA Modules:
  0.0 175.7 jit_solution(8022159265524445045)
XLA Ops:
  0.6 0.0 copy-start
  0.6 0.7 copy-done
  1.3 4.0 %local_mix.1 = f32[8,16,32,256]{3,2,1,0:T(8,128)S(1)} custom-call(f32[4096,256]{1,0:T(8,128)} %refs_0_.1, s32[32,128]{1,0:T(8,128)S(1)} %bitcast.7), custom_call_target="tpu_custom_call" | custom-call | tf_op jit(solution)/shard_map/local_mix/pallas_call | solution.py:122
  5.4 64.0 %all_to_all.20.in_ref = f32[128,32,256]{2,1,0:T(8,128)S(1)} all-to-all(f32[128,32,256]{2,1,0:T(8,128)S(1)} %bitcast.6), channel_id=1, replica_groups=mesh['y_low'=2,'x'=4,'z'=4,'core'=2,'y_high'=2] {'z','core','x','y_high'..., dimensions={0} | all-to-all | bytes 8388608 | tf_op jit(solution)/shard_map/all_to_all | solution.py:374
  69.4 1.7 across_mix.1
  71.1 0.0 copy-start.1
  71.1 56.7 %all_to_all.21.values_ref.refs_2_ = f32[128,2,32,128]{3,2,1,0:T(8,128)S(1)} all-to-all(f32[128,2,32,128]{3,2,1,0:T(8,128)S(1)} %across_mix.1), channel_id=1, replica_groups=mesh['y_low'=2,'x'=4,'z'=4,'core'=2,'y_high'=2] {'z','core','x','y_high'..., dimensions={0} | all-to-all | bytes 8388608 | tf_op jit(solution)/shard_map/all_to_all | solution.py:374
  127.8 0.0 copy-done.1
  127.8 3.1 %pick_rows.1 = f32[128,3,4,128]{3,2,1,0:T(4,128)S(1)} custom-call(s32[4,128]{1,0:T(4,128)S(1)} %bitcast.8, f32[128,2,32,128]{3,2,1,0:T(8,128)S(1)} %all_to_all.21.values_ref.refs_2_), custom_call_target="tpu_custom_call" | custom-call | tf_op jit(solution)/shard_map/pick_rows/pallas_call | solution.py:239
  130.9 20.0 %all_to_all.22.refs_1_ = f32[128,3,4,128]{3,2,1,0:T(4,128)S(1)} all-to-all(f32[128,3,4,128]{3,2,1,0:T(4,128)S(1)} %pick_rows.1), channel_id=1, replica_groups=mesh['y_low'=2,'x'=4,'z'=4,'core'=2,'y_high'=2] {'z','core','x','y_high'..., dimensions={0} | all-to-all | bytes 1572864 | tf_op jit(solution)/shard_map/all_to_all | solution.py:374
  150.9 0.1 slice_reduce_fusion
  151.1 15.5 %all_to_all.23.refs_0_ = f32[128,4,128]{2,1,0:T(4,128)S(1)} all-to-all(f32[128,4,128]{2,1,0:T(4,128)S(1)} %broadcast_in_dim.3), channel_id=1, replica_groups=mesh['y_low'=2,'x'=4,'z'=4,'core'=2,'y_high'=2] {'z','core','x','y_high'..., dimensions={0} | all-to-all | bytes 524288 | tf_op jit(solution)/shard_map/all_to_all | solution.py:374
  166.6 9.1 %finish.1 = (f32[128,32,256]{2,1,0:T(8,128)}, f32[512,256]{1,0:T(8,128)}, f32[256,256]{1,0:T(8,128)}) custom-call(f32[128,4,128]{2,1,0:T(4,128)S(1)} %all_to_all.23.refs_0_, f32[128,3,4,128]{3,2,1,0:T(4,128)S(1)} %all_to_all.22.refs_1_, f32[128,2,32,128]{3,2,1,0:T(8,128)S(1)} %all_to_all.21.values_ref.refs_2_), custom_call_target="tpu_custom_call" | custom-call | tf_op jit(solution)/shard_map/finish/pallas_call | solution.py:354
  (1 shorter events, 0.0 us)
Async XLA Ops:
  0.6 0.7 copy-start
  71.1 56.7 %copy-start.1 = (s32[1,128,4]{1,2,0:T(4,128)S(1)}, s32[1,128,4]{1,2,0:T(4,128)}, u32[]{:S(2)}) copy-start(s32[1,128,4]{1,2,0:T(4,128)} %param.5) | copy-start | bytes 6148

commit v7 on v6

--- a/solution.py
+++ b/solution.py
@@ -202,7 +202,8 @@
 def pick_kernel(picks_ref, values_ref, out_ref, taken):
     count, halves, rows, width = values_ref.shape
     tiles, _, slots, _ = taken.shape
-    owners, _, each, _ = out_ref.shape
+    owners = out_ref.shape[0]
+    each = picks_ref.shape[0]
     shift = rows.bit_length() - 1
     flat = values_ref.reshape(count * halves * rows, width)
 
@@ -218,19 +219,20 @@
                 for half in range(halves):
                     part = jnp.where(pick >= 0, flat[pl.ds(at + half * rows, 1), :], 0.0)
                     taken[tile, half, slot:slot + 1, :] = part
-                    out_ref[first + turn(pair), half, place:place + 1, :] = part
+                    out_ref[first + turn(pair), half * each + place] = part
         return carry
 
     lax.fori_loop(0, tiles // AT_ONCE, body, 0)
     panel = jnp.concatenate([taken[:, half].reshape(-1, 128) for half in range(halves)], axis=1)
     left, right = factors(split(panel.T), split(panel), 1)
     gram = jnp.dot(left, right, preferred_element_type=jnp.float32)
-    each = gram.shape[0] // out_ref.shape[0]
-    for owner in range(out_ref.shape[0]):
-        for half in range(halves):
-            out_ref[owner, halves, half * each:(half + 1) * each, :] = (
-                gram[owner * each:(owner + 1) * each, half * 128:half * 128 + 128]
-            )
+    for owner in range(owners):
+        line = halves * each
+        for top in range(halves):
+            for half in range(top, halves):
+                row = top * width + owner
+                out_ref[owner, line] = gram[row:row + 1, half * 128:half * 128 + 128]
+                line += 1
 
 
 def pick_rows(values, picks):
@@ -238,7 +240,7 @@
     slots, owners = picks.shape
     return pl.pallas_call(
         pick_kernel,
-        out_shape=jax.ShapeDtypeStruct((owners, halves + 1, slots, 128), jnp.float32),
+        out_shape=jax.ShapeDtypeStruct((owners, halves * slots + halves * (halves + 1) // 2, 1, 128), jnp.float32),
         in_specs=[whole(pltpu.SMEM), whole()],
         out_specs=whole(),
         scratch_shapes=[pltpu.VMEM((slots * owners // TILE, halves, TILE, 128), jnp.float32)],
@@ -250,7 +252,6 @@
 def finish_kernel(expected, pieces_ref, received_ref, values_ref, mixed_ref, panel_ref, out_ref, held, panel, sems):
     size = held.shape[0]
     halves = size // 128
-    each = pieces_ref.shape[1] // halves
     copies = [
         pltpu.make_async_copy(
             values_ref.at[:, half], mixed_ref.at[:, :, half * 128:half * 128 + 128], sems.at[half]
@@ -260,21 +261,26 @@
     copies.append(pltpu.make_async_copy(panel, panel_ref, sems.at[halves]))
     for copy in copies[:halves]:
         copy.start()
-    sources, _, slots, _ = received_ref.shape
+    sources = received_ref.shape[0]
+    slots = panel.shape[0] // sources
 
     def move_rows(owner):
-        for half in range(halves):
-            held[owner * each:(owner + 1) * each, half * 128:half * 128 + 128] = (
-                pieces_ref[owner, half * each:(half + 1) * each, :] * (1.0 / expected)
-            )
+        line = 0
+        for top in range(halves):
+            for half in range(top, halves):
+                row = top * 128 + owner
+                held[row:row + 1, half * 128:half * 128 + 128] = pieces_ref[owner, line] * (1.0 / expected)
+                line += 1
 
     def move_panel(source):
         for half in range(halves):
-            panel[source * slots:(source + 1) * slots, half * 128:half * 128 + 128] = (
-                received_ref[turn(source), half]
-            )
-
-    first_owners = SUPER // each
+            for slot in range(slots):
+                row = source * slots + slot
+                panel[row:row + 1, half * 128:half * 128 + 128] = received_ref[turn(source), half * slots + slot]
+
+    held[128:, :128] = jnp.zeros((size - 128, 128), jnp.float32)
+
+    first_owners = SUPER
     for owner in range(first_owners):
         move_rows(owner)
     moves = [(move_rows, owner) for owner in range(first_owners, pieces_ref.shape[0])]
@@ -347,10 +353,10 @@
 
 
 def finish(pieces, received, values, expected):
-    owners, rows, width = pieces.shape
-    count, halves, share, _ = values.shape
+    count, halves, share, width = values.shape
     size = halves * width
-    panel = jax.ShapeDtypeStruct((received.shape[0] * received.shape[2], size), jnp.float32)
+    slots = (received.shape[1] - pieces.shape[1]) // halves
+    panel = jax.ShapeDtypeStruct((received.shape[0] * slots, size), jnp.float32)
     return pl.pallas_call(
         lambda *refs: finish_kernel(expected, *refs),
         out_shape=(
@@ -383,7 +389,7 @@
 
     values = exchange(across_mix(exchange(local_mix(matrix_rows, signs, scale, owners))))
     received = exchange(pick_rows(values, picks[0].T))
-    piece = jnp.sum(received[:, -1], axis=0)
+    piece = jnp.sum(received[:, slots * width // 128:], axis=0)
     pieces = exchange(jnp.broadcast_to(piece, (owners,) + piece.shape))
     mixed, panel, factor = finish(pieces, received, values, expected)
     return (mixed.reshape(length, width), panel, factor)

time: 176 us -> 175 us (level)
  no operation moved by 1% of the time
where the time goes in v7:
time: 175 us
  blocking collectives  155 us (89%)
  Pallas kernels  17.9 us (10%)
    all_to_all x4, blocking collectives, exchange(): return lax.all_to_all(block, ROUND, split_axis=0, concat_axis=0, tiled=True)  155 us
    pallas_call x1, Pallas kernels, finish(): pl.pallas_call(lambda *refs: finish_kernel(expected, *refs), out_shape=(j...  9.05 us
    pallas_call x1, Pallas kernels, local_mix(): pl.pallas_call(lambda *refs: local_kernel(scale, *refs), out_shape=jax.Sh...  4.04 us

profile of v7, /device:TPU:1, one launch (start us, length us, event | category | flops | bytes accessed | tf_op | source)
XLA Modules:
  0.0 174.7 jit_solution(10218538915201578599)
XLA Ops:
  0.6 0.0 copy-start
  0.6 0.7 copy-done
  1.3 4.0 %local_mix.1 = f32[8,16,32,256]{3,2,1,0:T(8,128)S(1)} custom-call(f32[4096,256]{1,0:T(8,128)} %refs_0_.1, s32[32,128]{1,0:T(8,128)S(1)} %bitcast.7), custom_call_target="tpu_custom_call" | custom-call | tf_op jit(solution)/shard_map/local_mix/pallas_call | solution.py:122
  5.4 64.0 %all_to_all.20.in_ref = f32[128,32,256]{2,1,0:T(8,128)S(1)} all-to-all(f32[128,32,256]{2,1,0:T(8,128)S(1)} %bitcast.6), channel_id=1, replica_groups=mesh['y_low'=2,'x'=4,'z'=4,'core'=2,'y_high'=2] {'z','core','x','y_high'..., dimensions={0} | all-to-all | bytes 8388608 | tf_op jit(solution)/shard_map/all_to_all | solution.py:380
  69.4 1.7 across_mix.1
  71.1 0.0 copy-start.1
  71.1 56.7 %all_to_all.21.values_ref.refs_2_ = f32[128,2,32,128]{3,2,1,0:T(8,128)S(1)} all-to-all(f32[128,2,32,128]{3,2,1,0:T(8,128)S(1)} %across_mix.1), channel_id=1, replica_groups=mesh['y_low'=2,'x'=4,'z'=4,'core'=2,'y_high'=2] {'z','core','x','y_high'..., dimensions={0} | all-to-all | bytes 8388608 | tf_op jit(solution)/shard_map/all_to_all | solution.py:380
  127.8 0.0 copy-done.1
  127.8 3.2 %pick_rows.1 = f32[128,11,1,128]{3,2,1,0:T(1,128)S(1)} custom-call(s32[4,128]{1,0:T(4,128)S(1)} %bitcast.8, f32[128,2,32,128]{3,2,1,0:T(8,128)S(1)} %all_to_all.21.values_ref.refs_2_), custom_call_target="tpu_custom_call" | custom-call | tf_op jit(solution)/shard_map/pick_rows/pallas_call | solution.py:241
  130.9 19.4 %all_to_all.22.refs_1_ = f32[128,11,1,128]{3,2,1,0:T(1,128)S(1)} all-to-all(f32[128,11,1,128]{3,2,1,0:T(1,128)S(1)} %pick_rows.1), channel_id=1, replica_groups=mesh['y_low'=2,'x'=4,'z'=4,'core'=2,'y_high'=2] {'z','core','x','y_high'..., dimensions={0} | all-to-all | bytes 1441792 | tf_op jit(solution)/shard_map/all_to_all | solution.py:380
  150.3 0.2 slice_reduce_fusion
  150.5 0.1 broadcast_in_dim.3
  150.6 14.9 %all_to_all.23.refs_0_ = f32[128,3,1,128]{3,2,1,0:T(1,128)S(1)} all-to-all(f32[128,3,1,128]{3,2,1,0:T(1,128)S(1)} %broadcast_in_dim.3), channel_id=1, replica_groups=mesh['y_low'=2,'x'=4,'z'=4,'core'=2,'y_high'=2] {'z','core','x','y_high'..., dimensions={0} | all-to-all | bytes 393216 | tf_op jit(solution)/shard_map/all_to_all | solution.py:380
  165.5 9.0 %finish.1 = (f32[128,32,256]{2,1,0:T(8,128)}, f32[512,256]{1,0:T(8,128)}, f32[256,256]{1,0:T(8,128)}) custom-call(f32[128,3,1,128]{3,2,1,0:T(1,128)S(1)} %all_to_all.23.refs_0_, f32[128,11,1,128]{3,2,1,0:T(1,128)S(1)} %all_to_all.22.refs_1_, f32[128,2,32,128]{3,2,1,0:T(8,128)S(1)} %all_to_all.21.values_ref.refs_2_), custom_call_target="tpu_custom_call" | custom-call | tf_op jit(solution)/shard_map/finish/pallas_call | solution.py:360
Async XLA Ops:
  0.6 0.7 copy-start
  71.1 56.7 %copy-start.1 = (s32[1,128,4]{1,2,0:T(4,128)S(1)}, s32[1,128,4]{1,2,0:T(4,128)}, u32[]{:S(2)}) copy-start(s32[1,128,4]{1,2,0:T(4,128)} %param.5) | copy-start | bytes 6148

commit v8 on v7

--- a/solution.py
+++ b/solution.py
@@ -13,7 +13,7 @@
 TILE = 8
 RADIX = 8
 AT_ONCE = 16
-MOVES = 4
+MOVES = 1
 SUPER = 64
 VMEM = 40 * 2**20
 SMALL = 16 * 2**20
@@ -304,6 +304,7 @@
         for t in range(tiles):
             first = base + t * TILE
             half, column = first // 128, first % 128
+            low = half
             edges = {
                 u: [spread_column(rows[u][half], column + k) for k in range(TILE)]
                 for u in range(t, tiles)
@@ -317,9 +318,9 @@
                 inverse = 1.0 / pivot
                 root = lax.rsqrt(pivot)
                 root = root * (1.5 - 0.5 * pivot * root * root)
-                lines = [spread_row(rows[t][h], k) for h in range(halves)]
+                lines = [spread_row(rows[t][h], k) if h >= low else rows[t][h] for h in range(halves)]
                 finished = [
-                    jnp.where(place == k, lines[h] * root, finished[h]) for h in range(halves)
+                    jnp.where(place == k, lines[h] * root, finished[h]) if h >= low else finished[h] for h in range(halves)
                 ]
                 lines = [line * inverse for line in lines]
                 weights = [None] * TILE
@@ -329,14 +330,14 @@
                     edge = edges[u][k]
                     for m in range(k + 1, TILE):
                         edges[u][m] = edges[u][m] - edge * weights[m]
-                    for h in range(halves):
+                    for h in range(low, halves):
                         rows[u][h] = rows[u][h] - edge * lines[h]
             rows[t] = [
                 jnp.where(lane + h * 128 >= first + place, finished[h], 0.0) for h in range(halves)
             ]
             for h in range(halves):
                 out_ref[first:first + TILE, h * 128:h * 128 + 128] = rows[t][h]
-        if base == 0:
+        if base == size // 2:
             for move, number in moves:
                 move(number)
             moves = []

time: 175 us -> 175 us (level)
  no operation moved by 1% of the time
where the time goes in v8:
time: 175 us
  blocking collectives  155 us (89%)
  Pallas kernels  17.9 us (10%)
    all_to_all x4, blocking collectives, exchange(): return lax.all_to_all(block, ROUND, split_axis=0, concat_axis=0, tiled=True)  155 us
    pallas_call x1, Pallas kernels, finish(): pl.pallas_call(lambda *refs: finish_kernel(expected, *refs), out_shape=(j...  9.05 us
    pallas_call x1, Pallas kernels, local_mix(): pl.pallas_call(lambda *refs: local_kernel(scale, *refs), out_shape=jax.Sh...  4.04 us

profile of v8, /device:TPU:1, one launch (start us, length us, event | category | flops | bytes accessed | tf_op | source)
XLA Modules:
  0.0 174.7 jit_solution(10218538915201578599)
XLA Ops:
  0.6 0.0 copy-start
  0.6 0.7 copy-done
  1.3 4.0 %local_mix.1 = f32[8,16,32,256]{3,2,1,0:T(8,128)S(1)} custom-call(f32[4096,256]{1,0:T(8,128)} %refs_0_.1, s32[32,128]{1,0:T(8,128)S(1)} %bitcast.7), custom_call_target="tpu_custom_call" | custom-call | tf_op jit(solution)/shard_map/local_mix/pallas_call | solution.py:122
  5.4 64.0 %all_to_all.20.in_ref = f32[128,32,256]{2,1,0:T(8,128)S(1)} all-to-all(f32[128,32,256]{2,1,0:T(8,128)S(1)} %bitcast.6), channel_id=1, replica_groups=mesh['y_low'=2,'x'=4,'z'=4,'core'=2,'y_high'=2] {'z','core','x','y_high'..., dimensions={0} | all-to-all | bytes 8388608 | tf_op jit(solution)/shard_map/all_to_all | solution.py:381
  69.4 1.7 across_mix.1
  71.1 0.0 copy-start.1
  71.1 56.7 %all_to_all.21.values_ref.refs_2_ = f32[128,2,32,128]{3,2,1,0:T(8,128)S(1)} all-to-all(f32[128,2,32,128]{3,2,1,0:T(8,128)S(1)} %across_mix.1), channel_id=1, replica_groups=mesh['y_low'=2,'x'=4,'z'=4,'core'=2,'y_high'=2] {'z','core','x','y_high'..., dimensions={0} | all-to-all | bytes 8388608 | tf_op jit(solution)/shard_map/all_to_all | solution.py:381
  127.8 0.0 copy-done.1
  127.8 3.2 %pick_rows.1 = f32[128,11,1,128]{3,2,1,0:T(1,128)S(1)} custom-call(s32[4,128]{1,0:T(4,128)S(1)} %bitcast.8, f32[128,2,32,128]{3,2,1,0:T(8,128)S(1)} %all_to_all.21.values_ref.refs_2_), custom_call_target="tpu_custom_call" | custom-call | tf_op jit(solution)/shard_map/pick_rows/pallas_call | solution.py:241
  130.9 19.4 %all_to_all.22.refs_1_ = f32[128,11,1,128]{3,2,1,0:T(1,128)S(1)} all-to-all(f32[128,11,1,128]{3,2,1,0:T(1,128)S(1)} %pick_rows.1), channel_id=1, replica_groups=mesh['y_low'=2,'x'=4,'z'=4,'core'=2,'y_high'=2] {'z','core','x','y_high'..., dimensions={0} | all-to-all | bytes 1441792 | tf_op jit(solution)/shard_map/all_to_all | solution.py:381
  150.3 0.2 slice_reduce_fusion
  150.5 0.1 broadcast_in_dim.3
  150.6 14.9 %all_to_all.23.refs_0_ = f32[128,3,1,128]{3,2,1,0:T(1,128)S(1)} all-to-all(f32[128,3,1,128]{3,2,1,0:T(1,128)S(1)} %broadcast_in_dim.3), channel_id=1, replica_groups=mesh['y_low'=2,'x'=4,'z'=4,'core'=2,'y_high'=2] {'z','core','x','y_high'..., dimensions={0} | all-to-all | bytes 393216 | tf_op jit(solution)/shard_map/all_to_all | solution.py:381
  165.5 9.0 %finish.1 = (f32[128,32,256]{2,1,0:T(8,128)}, f32[512,256]{1,0:T(8,128)}, f32[256,256]{1,0:T(8,128)}) custom-call(f32[128,3,1,128]{3,2,1,0:T(1,128)S(1)} %all_to_all.23.refs_0_, f32[128,11,1,128]{3,2,1,0:T(1,128)S(1)} %all_to_all.22.refs_1_, f32[128,2,32,128]{3,2,1,0:T(8,128)S(1)} %all_to_all.21.values_ref.refs_2_), custom_call_target="tpu_custom_call" | custom-call | tf_op jit(solution)/shard_map/finish/pallas_call | solution.py:361
Async XLA Ops:
  0.6 0.7 copy-start
  71.1 56.7 %copy-start.1 = (s32[1,128,4]{1,2,0:T(4,128)S(1)}, s32[1,128,4]{1,2,0:T(4,128)}, u32[]{:S(2)}) copy-start(s32[1,128,4]{1,2,0:T(4,128)} %param.5) | copy-start | bytes 6148

commit v9 on v7

--- a/solution.py
+++ b/solution.py
@@ -112,7 +112,7 @@
                     out_ref[c, q, t * TILE:(t + 1) * TILE, h * 128:h * 128 + 128] = parts[c]
         return carry
 
-    lax.fori_loop(0, size // share, last, 0, unroll=2)
+    lax.fori_loop(0, size // share, last, 0, unroll=4)
 
 
 def local_mix(matrix_rows, signs, scale, owners):
@@ -155,7 +155,7 @@
                     out_ref[group * inner + b, half, pl.ds(at, 8), :] = parts[b]
         return carry
 
-    lax.fori_loop(0, rows // 8, body, 0)
+    lax.fori_loop(0, rows // 8, body, 0, unroll=4)
 
 
 def across_mix(values):

time: 175 us -> 175 us (level)
  no operation moved by 1% of the time
where the time goes in v9:
time: 175 us
  blocking collectives  155 us (89%)
  Pallas kernels  17.9 us (10%)
    all_to_all x4, blocking collectives, exchange(): return lax.all_to_all(block, ROUND, split_axis=0, concat_axis=0, tiled=True)  155 us
    pallas_call x1, Pallas kernels, finish(): pl.pallas_call(lambda *refs: finish_kernel(expected, *refs), out_shape=(j...  9.05 us
    pallas_call x1, Pallas kernels, local_mix(): pl.pallas_call(lambda *refs: local_kernel(scale, *refs), out_shape=jax.Sh...  4.02 us

profile of v9, /device:TPU:1, one launch (start us, length us, event | category | flops | bytes accessed | tf_op | source)
XLA Modules:
  0.0 174.7 jit_solution(18085525899370389810)
XLA Ops:
  0.6 0.0 copy-start
  0.6 0.7 copy-done
  1.3 4.0 %local_mix.1 = f32[8,16,32,256]{3,2,1,0:T(8,128)S(1)} custom-call(f32[4096,256]{1,0:T(8,128)} %refs_0_.1, s32[32,128]{1,0:T(8,128)S(1)} %bitcast.7), custom_call_target="tpu_custom_call" | custom-call | tf_op jit(solution)/shard_map/local_mix/pallas_call | solution.py:122
  5.4 64.0 %all_to_all.20.in_ref = f32[128,32,256]{2,1,0:T(8,128)S(1)} all-to-all(f32[128,32,256]{2,1,0:T(8,128)S(1)} %bitcast.6), channel_id=1, replica_groups=mesh['y_low'=2,'x'=4,'z'=4,'core'=2,'y_high'=2] {'z','core','x','y_high'..., dimensions={0} | all-to-all | bytes 8388608 | tf_op jit(solution)/shard_map/all_to_all | solution.py:380
  69.3 1.7 across_mix.1
  71.0 0.0 copy-start.1
  71.1 56.7 %all_to_all.21.values_ref.refs_2_ = f32[128,2,32,128]{3,2,1,0:T(8,128)S(1)} all-to-all(f32[128,2,32,128]{3,2,1,0:T(8,128)S(1)} %across_mix.1), channel_id=1, replica_groups=mesh['y_low'=2,'x'=4,'z'=4,'core'=2,'y_high'=2] {'z','core','x','y_high'..., dimensions={0} | all-to-all | bytes 8388608 | tf_op jit(solution)/shard_map/all_to_all | solution.py:380
  127.8 0.0 copy-done.1
  127.8 3.2 %pick_rows.1 = f32[128,11,1,128]{3,2,1,0:T(1,128)S(1)} custom-call(s32[4,128]{1,0:T(4,128)S(1)} %bitcast.8, f32[128,2,32,128]{3,2,1,0:T(8,128)S(1)} %all_to_all.21.values_ref.refs_2_), custom_call_target="tpu_custom_call" | custom-call | tf_op jit(solution)/shard_map/pick_rows/pallas_call | solution.py:241
  130.9 19.4 %all_to_all.22.refs_1_ = f32[128,11,1,128]{3,2,1,0:T(1,128)S(1)} all-to-all(f32[128,11,1,128]{3,2,1,0:T(1,128)S(1)} %pick_rows.1), channel_id=1, replica_groups=mesh['y_low'=2,'x'=4,'z'=4,'core'=2,'y_high'=2] {'z','core','x','y_high'..., dimensions={0} | all-to-all | bytes 1441792 | tf_op jit(solution)/shard_map/all_to_all | solution.py:380
  150.3 0.2 slice_reduce_fusion
  150.5 0.1 broadcast_in_dim.3
  150.6 14.9 %all_to_all.23.refs_0_ = f32[128,3,1,128]{3,2,1,0:T(1,128)S(1)} all-to-all(f32[128,3,1,128]{3,2,1,0:T(1,128)S(1)} %broadcast_in_dim.3), channel_id=1, replica_groups=mesh['y_low'=2,'x'=4,'z'=4,'core'=2,'y_high'=2] {'z','core','x','y_high'..., dimensions={0} | all-to-all | bytes 393216 | tf_op jit(solution)/shard_map/all_to_all | solution.py:380
  165.5 9.0 %finish.1 = (f32[128,32,256]{2,1,0:T(8,128)}, f32[512,256]{1,0:T(8,128)}, f32[256,256]{1,0:T(8,128)}) custom-call(f32[128,3,1,128]{3,2,1,0:T(1,128)S(1)} %all_to_all.23.refs_0_, f32[128,11,1,128]{3,2,1,0:T(1,128)S(1)} %all_to_all.22.refs_1_, f32[128,2,32,128]{3,2,1,0:T(8,128)S(1)} %all_to_all.21.values_ref.refs_2_), custom_call_target="tpu_custom_call" | custom-call | tf_op jit(solution)/shard_map/finish/pallas_call | solution.py:360
Async XLA Ops:
  0.6 0.7 copy-start
  71.0 56.7 %copy-start.1 = (s32[1,128,4]{1,2,0:T(4,128)S(1)}, s32[1,128,4]{1,2,0:T(4,128)}, u32[]{:S(2)}) copy-start(s32[1,128,4]{1,2,0:T(4,128)} %param.5) | copy-start | bytes 6148
